TPU v7x, 256 devices: a whole 4x4x8 slice. The times are simulated.
256 devices in a mesh: dp: 4 (over y_hi, core), expert: 64 (over z, x, y_lo).
Axes of the slice: x: 4, y: 4 (y_hi: 2, y_lo: 2; y = y_hi * 2 + y_lo), z: 8, core: 2. Of those that a mesh axis runs over, the one named last changes fastest.
Arguments:
- tokens: bfloat16 [512, 256, 1024], P(('dp', 'expert')), may hold values from -20 to 20
- slot_params: bfloat16 [1024, 128], replicated, may hold values from -1 to 1
- w_in: bfloat16 [128, 1024, 2560], P('expert', None, 'dp'), may hold values from -0.1875 to 0.1875
- w_out: bfloat16 [128, 2560, 1024], P('expert', 'dp'), may hold values from -0.125 to 0.125
- slot_outputs: bfloat16 [512, 128, 1024], P(('dp', 'expert')), may hold values from -6 to 6
- out_grad: bfloat16 [512, 256, 1024], P(('dp', 'expert')), may hold values from -24 to 24
Outputs:
- tokens_grad: bfloat16 [512, 256, 1024], P(('dp', 'expert'))
- params_grad: float32 [1024, 128], replicated
- w_in_grad: bfloat16 [128, 1024, 2560], P('expert', None, 'dp')
- w_out_grad: bfloat16 [128, 2560, 1024], P('expert', 'dp')
All inputs are finite; a program needn't handle non-finite values.
Results may differ from a plain program's by a relative error of at most 0.017.
Values may be sent and summed in bfloat16 or wider, within the bound.
No kernel may reach another device: no remote copies, remote signals or barrier semaphores. Data moves between devices by JAX's collectives and lax.ppermute only.
A program may use at most 128 MiB of HBM per device.

v0:
```python
import functools

import jax
import jax.numpy as jnp
from jax import lax
from jax.experimental import pallas as pl
from jax.experimental.pallas import tpu as pltpu
from jax.sharding import Mesh, PartitionSpec as P

inv_root_two = 0.7071067811865476
inv_root_tau = 0.3989422804014327

bf16 = jnp.bfloat16
f32 = jnp.float32
Y = ("yh", "yl")
ZX = ("z", "x")
CORE_SWAP = [(0, 1), (1, 0)]
MIB = 1 << 20


def dot(a, b, dims=((1,), (0,))):
    return lax.dot_general(a, b, (dims, ((), ())), preferred_element_type=f32)


def one_hot(test):
    return jnp.where(test, 1.0, 0.0).astype(bf16)


def message_rows(shape, axis, yl, frames):
    row = lax.broadcasted_iota(jnp.int32, shape, axis)
    frame = row & (frames - 1)
    rest = row // frames
    expert = (rest // 4) * 4 + ((((rest // 2) & 1) ^ yl) * 2) + (rest & 1)
    return frame * (shape[axis] // frames) + expert


def call(kernel, out_shape, *args, grid=(), in_specs=None, out_specs=None, vmem=16, flops=0, **kw):
    nbytes = sum(a.size * a.dtype.itemsize for a in args)
    nbytes += sum(o.size * o.dtype.itemsize for o in jax.tree.leaves(out_shape))
    if in_specs is None:
        in_specs = [pl.BlockSpec(memory_space=pltpu.VMEM) for _ in args]
    if out_specs is None:
        out_specs = jax.tree.map(lambda _: pl.BlockSpec(memory_space=pltpu.VMEM), out_shape)
    return pl.pallas_call(
        kernel,
        out_shape=out_shape,
        grid=grid,
        in_specs=in_specs,
        out_specs=out_specs,
        compiler_params=pltpu.CompilerParams(vmem_limit_bytes=vmem * MIB),
        cost_estimate=pl.CostEstimate(flops=flops, bytes_accessed=nbytes, transcendentals=0),
        **kw,
    )(*args)


def shape(dims, dtype):
    return jax.ShapeDtypeStruct(dims, dtype)


SMEM = pl.BlockSpec(memory_space=pltpu.SMEM)
VMEM = pl.BlockSpec(memory_space=pltpu.VMEM)
ANY = pl.BlockSpec(memory_space=pl.ANY)


def to_message(place_ref, slots, out_ref):
    rows = out_ref.shape[0]
    yl = place_ref[0]
    order = one_hot(
        message_rows((rows, rows), 0, yl, len(slots)) == lax.broadcasted_iota(jnp.int32, (rows, rows), 1)
    )
    out_ref[...] = dot(order, jnp.concatenate(slots, axis=0)).astype(bf16)


def prep_kernel(place_ref, tokens_ref, params_ref, message_ref, dispatch_ref, combine_ref):
    slots = []
    for f in range(tokens_ref.shape[0]):
        tokens = tokens_ref[f]
        logits = dot(tokens, params_ref[...])
        up = jnp.exp(logits - jnp.max(logits, axis=0, keepdims=True))
        dispatch = up / jnp.sum(up, axis=0, keepdims=True)
        dispatch_ref[f] = dispatch
        slots.append(dot(dispatch.astype(bf16), tokens, ((0,), (0,))).astype(bf16))
        up = jnp.exp(logits - jnp.max(logits, axis=1, keepdims=True))
        combine_ref[f] = up / jnp.sum(up, axis=1, keepdims=True)
    to_message(place_ref, slots, message_ref)


def grad_kernel(place_ref, combine_ref, out_grad_ref, message_ref):
    slots = []
    for f in range(out_grad_ref.shape[0]):
        low = combine_ref[f].astype(bf16)
        slots.append(dot(low, out_grad_ref[f], ((0,), (0,))).astype(bf16))
    to_message(place_ref, slots, message_ref)


def sort_order(rows, frames, axis):
    row = lax.broadcasted_iota(jnp.int32, (rows, rows), axis)
    pair = row // (rows // 4)
    rest = row - pair * (rows // 4)
    return (rest // frames) * (4 * frames) + pair * frames + (rest & (frames - 1))


def sort_kernel(frames, message_ref, own_ref, other_ref):
    rows, depth = message_ref.shape
    order = one_hot(
        sort_order(rows, frames, 0) == lax.broadcasted_iota(jnp.int32, (rows, rows), 1)
    )
    out = dot(order, message_ref[...]).astype(bf16)
    own_ref[...] = out[: rows // 2].reshape(own_ref.shape)
    other_ref[...] = out[rows // 2 :].reshape(other_ref.shape)


def unsort_kernel(frames, own_ref, across_ref, back_ref, ahead_ref, message_ref):
    rows, depth = message_ref.shape

    def total(a, b):
        value = a[...].astype(f32) + b[...].astype(f32)
        return value.reshape(rows // 2, depth).astype(bf16)

    value = jnp.concatenate([total(own_ref, across_ref), total(back_ref, ahead_ref)], axis=0)
    order = one_hot(
        sort_order(rows, frames, 1) == lax.broadcasted_iota(jnp.int32, (rows, rows), 0)
    )
    message_ref[...] = dot(order, value).astype(bf16)


def hidden_kernel(*refs):
    pieces, w_in_ref, rows_ref, hidden_ref = refs[:8], refs[8], refs[9], refs[10]
    rows = jnp.concatenate([piece[0] for piece in pieces], axis=0)
    rows_ref[0] = rows
    hidden_ref[0] = dot(rows, w_in_ref[0])


def expert_kernel(*refs):
    pieces, hidden_ref, w_in_ref, w_out_ref = refs[:4], refs[4], refs[5], refs[6]
    rows_ref, active_ref, pre_ref, partial_ref = refs[-4:]
    rows = jnp.concatenate([piece[0] for piece in pieces], axis=0)
    rows_ref[0] = rows
    hidden = hidden_ref[0]
    cdf = 0.5 * (1.0 + lax.erf(hidden * inv_root_two))
    dens = jnp.exp(-0.5 * hidden * hidden) * inv_root_tau
    active_ref[0] = (hidden * cdf).astype(bf16)
    act_grad = dot(rows, w_out_ref[0], ((1,), (1,)))
    pre = (act_grad * (cdf + hidden * dens)).astype(bf16)
    pre_ref[0] = pre
    partial = dot(pre, w_in_ref[0], ((1,), (1,)))
    partial_ref[...] = partial.astype(partial_ref.dtype).reshape(partial_ref.shape)


def tail_kernel(place_ref, message_ref, tokens_ref, dispatch_ref, part_ref, slots_ref, low_ref, mine_ref, theirs_ref, sum_ref):
    rows, depth = message_ref.shape
    frames, experts = slots_ref.shape[:2]
    order = one_hot(
        message_rows((rows, rows), 1, place_ref[0], frames)
        == lax.broadcasted_iota(jnp.int32, (rows, rows), 0)
    )
    slots = dot(order, message_ref[...]).astype(bf16)
    total = None
    for f in range(frames):
        mine = slots[f * experts : (f + 1) * experts]
        slots_ref[f] = mine
        tokens = tokens_ref[f]
        dispatch = dispatch_ref[f]
        slope = dot(tokens, mine, ((1,), (1,)))
        slope = slope - jnp.sum(dispatch * slope, axis=0, keepdims=True)
        low = (dispatch * slope + part_ref[f]).astype(bf16)
        low_ref[f] = low
        term = dot(low, tokens, ((0,), (0,)))
        total = term if total is None else total + term
    sum_ref[...] = total.T
    half = depth // 2
    core = place_ref[1]
    mine_ref[...] = sum_ref[pl.ds(pl.multiple_of(core * half, half), half), :]
    theirs_ref[...] = sum_ref[pl.ds(pl.multiple_of((1 - core) * half, half), half), :].astype(bf16)


def tokens_kernel(dispatch_ref, low_ref, slots_ref, params_ref, out_ref):
    params = params_ref[...].T
    for f in range(out_ref.shape[0]):
        left = jnp.concatenate([dispatch_ref[f].astype(bf16), low_ref[f]], axis=1)
        right = jnp.concatenate([slots_ref[f], params], axis=0)
        out_ref[f] = dot(left, right).astype(bf16)


def to_y(value, step):
    return lax.ppermute(value, Y, [(i, (i + step) % 4) for i in range(4)])


def to_core(value):
    return lax.ppermute(value, "core", CORE_SWAP)


def exchange(value):
    return lax.all_to_all(value, ZX, split_axis=0, concat_axis=0, tiled=True)


def spread(message, groups, frames):
    rows, depth = message.shape
    message = exchange(message.reshape(groups, rows // groups, depth)).reshape(rows, depth)
    half = shape((2, rows // 4, depth), bf16)
    own, other = call(
        functools.partial(sort_kernel, frames), (half, half), message, flops=2 * rows * rows * depth
    )
    near = [own, to_y(other, 1), to_y(other, -1), to_y(own, 2)]
    return near, [to_core(piece) for piece in near]


def sum_all(mine, theirs, groups, beside):
    half, cols = mine.shape
    core = lax.axis_index("core")
    mine = (mine + to_core(theirs).astype(f32)).astype(bf16)
    pieces = exchange(mine.reshape(groups, half // groups, cols))
    part = jnp.sum(pieces.astype(f32), axis=0)
    across, back, ahead = to_y(part, 2), to_y(part, 1), to_y(part, -1)
    across, beside = lax.optimization_barrier((across, beside))
    total = ((part + across) + (back + ahead)).astype(bf16)
    mine = exchange(jnp.broadcast_to(total[None], (groups,) + total.shape)).reshape(half, cols)
    theirs = to_core(mine)
    low = jnp.where(core == 0, mine, theirs)
    high = jnp.where(core == 0, theirs, mine)
    return jnp.concatenate([low, high], axis=0).astype(f32), beside


def shards(tokens, slot_params, w_in, w_out, slot_outputs, out_grad):
    frames, patch, depth = tokens.shape
    experts = slot_params.shape[1]
    hidden_size = w_in.shape[2]
    groups = experts // 4
    rows = frames * experts
    block = rows // 4
    place = jnp.stack([lax.axis_index("yl"), lax.axis_index("core")]).astype(jnp.int32)
    frame_flops = 2 * frames * patch * experts * depth
    sort_flops = 2 * rows * rows * depth

    message, dispatch, combine = call(
        prep_kernel,
        (
            shape((rows, depth), bf16),
            shape((frames, patch, experts), f32),
            shape((frames, patch, experts), f32),
        ),
        place, tokens, slot_params,
        in_specs=[SMEM, VMEM, VMEM], flops=2 * frame_flops + sort_flops,
    )
    near_in, far_in = spread(message, groups, frames)
    message = call(
        grad_kernel, shape((rows, depth), bf16), place, combine, out_grad,
        in_specs=[SMEM, VMEM, VMEM], flops=frame_flops + sort_flops,
    )
    near_grad, far_grad = spread(message, groups, frames)

    combine_grad = jnp.einsum(
        "fpd,fed->fpe", out_grad, slot_outputs, preferred_element_type=f32
    )
    combine_part = combine * (
        combine_grad - jnp.sum(combine * combine_grad, axis=2, keepdims=True)
    )

    piece = pl.BlockSpec((1, block, depth), lambda e: (e, 0, 0))
    w_in_spec = pl.BlockSpec((1, depth, hidden_size), lambda e: (e, 0, 0))
    w_out_spec = pl.BlockSpec((1, hidden_size, depth), lambda e: (e, 0, 0))
    matmul_flops = 2 * 2 * 8 * block * depth * hidden_size
    slot_rows, hidden = call(
        hidden_kernel,
        (shape((2, 8 * block, depth), bf16), shape((2, 8 * block, hidden_size), f32)),
        *near_in, *far_in, w_in,
        grid=(2,),
        in_specs=[piece] * 8 + [w_in_spec],
        out_specs=(
            pl.BlockSpec((1, 8 * block, depth), lambda e: (e, 0, 0)),
            pl.BlockSpec((1, 8 * block, hidden_size), lambda e: (e, 0, 0)),
        ),
        vmem=20, flops=matmul_flops,
    )

    hidden, combine_part = lax.optimization_barrier((hidden, combine_part))

    def expert_half(half, pieces, filled):
        rows_spec = pl.BlockSpec((1, 4 * block, depth), lambda e: (e, half, 0))
        hidden_spec = pl.BlockSpec((1, 4 * block, hidden_size), lambda e: (e, half, 0))
        return call(
            expert_kernel,
            (
                shape((2, 8 * block, depth), bf16),
                shape((2, 8 * block, hidden_size), bf16),
                shape((2, 8 * block, hidden_size), bf16),
                shape((4, 2, block, depth), bf16 if half else f32),
            ),
            *pieces, hidden, w_in, w_out, *filled,
            grid=(2,),
            in_specs=[piece] * 4 + [hidden_spec, w_in_spec, w_out_spec] + [ANY] * len(filled),
            out_specs=(
                rows_spec,
                hidden_spec,
                hidden_spec,
                pl.BlockSpec((4, 1, block, depth), lambda e: (0, e, 0, 0)),
            ),
            vmem=24, flops=matmul_flops,
            input_output_aliases={7 + i: i for i in range(len(filled))},
        )

    *filled, far = expert_half(1, far_grad, ())
    far = to_core(far)
    grad_rows, active, pre_grad, near = expert_half(0, near_grad, filled)

    def summed(i):
        return (near[i] + far[i].astype(f32)).astype(bf16)

    back, ahead, across, own = summed(1), summed(2), summed(3), summed(0)
    back, ahead, across = to_y(back, -1), to_y(ahead, 1), to_y(across, 2)
    w_out_grad = jnp.einsum(
        "erh,erd->ehd", active, grad_rows, preferred_element_type=f32
    ).astype(bf16)
    w_in_grad = jnp.einsum(
        "erd,erh->edh", slot_rows, pre_grad, preferred_element_type=f32
    ).astype(bf16)
    own, w_in_grad = lax.optimization_barrier((own, w_in_grad))
    message = call(
        functools.partial(unsort_kernel, frames), shape((rows, depth), bf16),
        own, across, back, ahead, flops=sort_flops,
    )
    message = exchange(message.reshape(groups, rows // groups, depth)).reshape(rows, depth)
    message, w_out_grad = lax.optimization_barrier((message, w_out_grad))

    slots_in_grad, logits_low, mine, theirs = call(
        tail_kernel,
        (
            shape((frames, experts, depth), bf16),
            shape((frames, patch, experts), bf16),
            shape((depth // 2, experts), f32),
            shape((depth // 2, experts), bf16),
        ),
        place, message, tokens, dispatch, combine_part,
        in_specs=[SMEM, VMEM, VMEM, VMEM, VMEM],
        scratch_shapes=[pltpu.VMEM((depth, experts), f32)],
        flops=2 * frame_flops + sort_flops,
    )
    tokens_grad = call(
        tokens_kernel, shape((frames, patch, depth), bf16),
        dispatch, logits_low, slots_in_grad, slot_params, flops=2 * frame_flops,
    )
    params_grad, tokens_grad = sum_all(mine, theirs, groups, tokens_grad)
    return (tokens_grad, params_grad, w_in_grad, w_out_grad)


def split_mesh(mesh):
    experts = mesh.devices.shape[1]
    x = 4 if experts >= 64 else 2
    return Mesh(
        mesh.devices.reshape(2, 2, experts // (2 * x), x, 2), ("yh", "core", "z", "x", "yl")
    )


def solution(mesh):
    dp, expert = ("yh", "core"), ("z", "x", "yl")
    whole = dp + expert
    in_specs = (
        P(whole, None, None),
        P(),
        P(expert, None, dp),
        P(expert, dp, None),
        P(whole, None, None),
        P(whole, None, None),
    )
    out_specs = (
        P(whole, None, None),
        P(),
        P(expert, None, dp),
        P(expert, dp, None),
    )
    return jax.shard_map(
        shards, mesh=split_mesh(mesh), in_specs=in_specs, out_specs=out_specs, check_vma=False
    )
```

profile of v0, /device:TPU:1, one launch (start us, length us, event | category | flops | bytes accessed | tf_op | source)
XLA Modules:
  0.0 192.2 jit_solution(8360612683637090399)
XLA Ops:
  3.0 2.7 %shard_map.93 = (bf16[256,1024]{1,0:T(8,128)(2,1)}, f32[2,256,128]{2,1,0:T(8,128)S(1)}, f32[2,256,128]{2,1,0:T(8,128)S(1)}) custom-call(s32[2]{0:T(128)S(1)} %pad_add_fusion.place_ref, bf16[2,256,1024]{2,1,0:T(8,128)(2,1)S(1)} %copy-done.12, bf16[1024,128]{1,0:T(8,128)(2,1)S(1)} %copy-done.14), custom_call_target="tpu_custom_call" | custom-call | flops 402653184 | bytes 2359304 | tf_op jit(solution)/shard_map/pallas_call | solution.py:44
  6.8 27.9 %all_to_all.25 = bf16[32,8,1024]{2,1,0:T(8,128)(2,1)S(1)} all-to-all(bf16[32,8,1024]{2,1,0:T(8,128)(2,1)S(1)} %bitcast.31), channel_id=1, replica_groups=mesh['yh'=2,'core'=2,'z'=8,'x'=4,'yl'=2] {'z','x'}, dimensions={0} | all-to-all | bytes 1048576 | tf_op jit(solution)/shard_map/all_to_all | solution.py:194
  34.8 5.2 %all-to-all-start.1 = ((bf16[32,8,1024]{2,1,0:T(8,128)(2,1)}), bf16[32,8,1024]{2,1,0:T(8,128)(2,1)S(1)}, u32[]{:S(2)}, u32[]{:S(2)}) async-start(bf16[32,8,1024]{2,1,0:T(8,128)(2,1)} %bitcast.4), calls=%async_computation.1 | async-start | bytes 1048576 | tf_op jit(solution)/shard_map/all_to_all | solution.py:194
  41.8 2.7 %collective-permute-start.1 = (bf16[2,64,1024]{2,1,0:T(8,128)(2,1)}, bf16[2,64,1024]{2,1,0:T(8,128)(2,1)}, u32[]{:S(2)}, u32[]{:S(2)}) collective-permute-start(bf16[2,64,1024]{2,1,0:T(8,128)(2,1)} %get-tuple-element.35), channel_id=1, source_target_pairs={{0,129},{1,0},{128,1},{129,128},{2,131},{3,2},{130,3},{131,130},{4... | collective-permute-start | bytes 786440 | tf_op jit(solution)/shard_map/ppermute | solution.py:186
  44.5 10.6 %all-to-all-done.1 = bf16[32,8,1024]{2,1,0:T(8,128)(2,1)S(1)} async-done(((bf16[32,8,1024]{2,1,0:T(8,128)(2,1)}), bf16[32,8,1024]{2,1,0:T(8,128)(2,1)S(1)}, u32[]{:S(2)}, u32[]{:S(2)}) %all-to-all-start.1) | async-done | bytes 524320 | tf_op jit(solution)/shard_map/all_to_all | solution.py:194
  57.3 2.8 %collective-permute-start.4 = (bf16[2,64,1024]{2,1,0:T(8,128)(2,1)S(1)}, bf16[2,64,1024]{2,1,0:T(8,128)(2,1)S(1)}, u32[]{:S(2)}, u32[]{:S(2)}) collective-permute-start(bf16[2,64,1024]{2,1,0:T(8,128)(2,1)S(1)} %get-tuple-element.38), channel_id=1, source_target_pairs={{0,129},{1,0},{128,1},{129,128},{2,131},{3,2},{130,3},{131,130},{4... | collective-permute-start | bytes 786440 | tf_op jit(solution)/shard_map/ppermute | solution.py:186
  61.7 4.6 %collective-permute-start.6 = (bf16[2,64,1024]{2,1,0:T(8,128)(2,1)S(1)}, bf16[2,64,1024]{2,1,0:T(8,128)(2,1)S(1)}, u32[]{:S(2)}, u32[]{:S(2)}) collective-permute-start(bf16[2,64,1024]{2,1,0:T(8,128)(2,1)S(1)} %get-tuple-element.37.refs_0_), channel_id=1, source_target_pairs={{0,64},{64,0},{1,65},{65,1},{2,66},{66,2},{3,67},{67,3},{4,68},{68... | collective-permute-start | bytes 786440 | tf_op jit(solution)/shard_map/ppermute | solution.py:190
  68.1 10.6 %collective-permute-start.8 = (bf16[2,64,1024]{2,1,0:T(8,128)(2,1)S(1)}, bf16[2,64,1024]{2,1,0:T(8,128)(2,1)S(1)}, u32[]{:S(2)}, u32[]{:S(2)}) collective-permute-start(bf16[2,64,1024]{2,1,0:T(8,128)(2,1)S(1)} %collective-permute-done.4.refs_2_), channel_id=1, source_target_pairs={{0,64},{64,0},{1,65},{65,1},{2,66},{66,2},{3,67},{67,3},{4,68},{68... | collective-permute-start | bytes 786440 | tf_op jit(solution)/shard_map/ppermute | solution.py:190
  85.1 2.6 %fusion.2.part_ref = f32[2,256,128]{2,1,0:T(8,128)S(1)} fusion(f32[2,256,128]{2,1,0:T(8,128)} %copy-done.9, bf16[2,256,1024]{2,1,0:T(8,128)(2,1)} %out_grad_ref.1, bf16[2,128,1024]{2,1,0:T(8,128)(2,1)S(1)} %copy-done), kind=kOutput, calls=%fused_computation.4 | convolution fusion | flops 268632704 | bytes 2097152 | tf_op jit(solution)/shard_map/sub | solution.py:256
  93.6 3.0 %shard_map.97 = (bf16[2,512,1024]{2,1,0:T(8,128)(2,1)S(1)}, f32[2,512,640]{2,1,0:T(8,128)S(1)}) custom-call(bf16[2,64,1024]{2,1,0:T(8,128)(2,1)S(1)} %copy-done.19, bf16[2,64,1024]{2,1,0:T(8,128)(2,1)S(1)} %copy-done.23, bf16[2,64,1024]{2,1,0:T(8,128)(2,1)S(1)} %copy-done.21, bf16[2,64,1024]{2,1,0:T(8,128)(2,1)} %collective-permute-done.5.refs_3_, ...), custom_call_target="tpu_custom_call" | custom-call | flops 1342177280 | bytes 9437184 | tf_op jit(solution)/shard_map/pallas_call | solution.py:44
  96.7 3.9 %shard_map.98 = (bf16[2,512,1024]{2,1,0:T(8,128)(2,1)S(1)}, bf16[2,512,640]{2,1,0:T(8,128)(2,1)S(1)}, bf16[2,512,640]{2,1,0:T(8,128)(2,1)S(1)}, bf16[4,2,64,1024]{3,2,1,0:T(8,128)(2,1)S(1)}) custom-call(bf16[2,64,1024]{2,1,0:T(8,128)(2,1)} %collective-permute-done.10.refs_0_, bf16[2,64,1024]{2,1,0:T(8,128)(2,1)} %collective-permute-done.11.refs_1_, ...), custom_call_target="tpu_custom_call" | custom-call | flops 1342177280 | bytes 14680064 | tf_op jit(solution)/shard_map/pallas_call | solution.py:44
  101.2 3.9 %shard_map.99 = (bf16[2,512,1024]{2,1,0:T(8,128)(2,1)S(1)}, bf16[2,512,640]{2,1,0:T(8,128)(2,1)S(1)}, bf16[2,512,640]{2,1,0:T(8,128)(2,1)S(1)}, f32[4,2,64,1024]{3,2,1,0:T(8,128)S(1)}) custom-call(bf16[2,64,1024]{2,1,0:T(8,128)(2,1)S(1)} %copy-done.17, ...), custom_call_target="tpu_custom_call", output_to_operand_aliasing={{0}: (7, {}), {1}: (8, {}), {2}: (9, {})} | custom-call | flops 1342177280 | bytes 20447232 | tf_op jit(solution)/shard_map/pallas_call | solution.py:44
  106.9 2.7 %collective-permute-start.16 = (bf16[2,64,1024]{2,1,0:T(8,128)(2,1)S(1)}, bf16[2,64,1024]{2,1,0:T(8,128)(2,1)S(1)}, u32[]{:S(2)}, u32[]{:S(2)}) collective-permute-start(bf16[2,64,1024]{2,1,0:T(8,128)(2,1)S(1)} %get-tuple-element.63), channel_id=1, source_target_pairs={{0,129},{1,0},{128,1},{129,128},{2,131},{3,2},{130,3},{131,130},{4... | collective-permute-start | bytes 786440 | tf_op jit(solution)/shard_map/ppermute | solution.py:186
  109.7 3.3 %convolution_convert_fusion.1 = bf16[2,1024,640]{2,1,0:T(8,128)(2,1)} fusion(bf16[2,512,1024]{2,1,0:T(8,128)(2,1)S(1)} %get-tuple-element.46, bf16[2,512,640]{2,1,0:T(8,128)(2,1)S(1)} %get-tuple-element.47), kind=kOutput, calls=%fused_computation.2 | convolution fusion | flops 1343488000 | bytes 6029312 | tf_op jit(solution)/shard_map/erd,erh->edh/dot_general | solution.py:314
  113.0 3.4 %collective-permute-done.17.ahead_ref = bf16[2,64,1024]{2,1,0:T(8,128)(2,1)S(1)} collective-permute-done((bf16[2,64,1024]{2,1,0:T(8,128)(2,1)S(1)}, bf16[2,64,1024]{2,1,0:T(8,128)(2,1)S(1)}, u32[]{:S(2)}, u32[]{:S(2)}) %collective-permute-start.17) | collective-permute-done | bytes 262176 | tf_op jit(solution)/shard_map/ppermute | solution.py:186
  116.4 4.0 %collective-permute-done.16.back_ref = bf16[2,64,1024]{2,1,0:T(8,128)(2,1)S(1)} collective-permute-done((bf16[2,64,1024]{2,1,0:T(8,128)(2,1)S(1)}, bf16[2,64,1024]{2,1,0:T(8,128)(2,1)S(1)}, u32[]{:S(2)}, u32[]{:S(2)}) %collective-permute-start.16) | collective-permute-done | bytes 262176 | tf_op jit(solution)/shard_map/ppermute | solution.py:186
  122.4 6.7 %all-to-all-start.2 = ((bf16[32,8,1024]{2,1,0:T(8,128)(2,1)}), bf16[32,8,1024]{2,1,0:T(8,128)(2,1)S(1)}, u32[]{:S(2)}, u32[]{:S(2)}) async-start(bf16[32,8,1024]{2,1,0:T(8,128)(2,1)} %bitcast.10), calls=%async_computation.2 | async-start | bytes 1048576 | tf_op jit(solution)/shard_map/all_to_all | solution.py:194
  129.2 4.4 %convolution_convert_fusion = bf16[2,640,1024]{2,1,0:T(8,128)(2,1)} fusion(bf16[2,512,640]{2,1,0:T(8,128)(2,1)} %copy-done.8, bf16[2,512,1024]{2,1,0:T(8,128)(2,1)S(1)} %copy-done.7), kind=kOutput, calls=%fused_computation.1 | convolution fusion | flops 1343488000 | bytes 6029312 | tf_op jit(solution)/shard_map/erh,erd->ehd/dot_general | solution.py:311
  133.6 11.1 %all-to-all-done.2 = bf16[32,8,1024]{2,1,0:T(8,128)(2,1)S(1)} async-done(((bf16[32,8,1024]{2,1,0:T(8,128)(2,1)}), bf16[32,8,1024]{2,1,0:T(8,128)(2,1)S(1)}, u32[]{:S(2)}, u32[]{:S(2)}) %all-to-all-start.2) | async-done | bytes 524320 | tf_op jit(solution)/shard_map/all_to_all | solution.py:194
  148.5 3.5 %collective-permute-start.18 = (bf16[512,128]{1,0:T(8,128)(2,1)S(1)}, bf16[512,128]{1,0:T(8,128)(2,1)S(1)}, u32[]{:S(2)}, u32[]{:S(2)}) collective-permute-start(bf16[512,128]{1,0:T(8,128)(2,1)S(1)} %get-tuple-element.55), channel_id=1, source_target_pairs={{0,64},{64,0},{1,65},{65,1},{2,66},{66,2},{3,67},{67,3},{4,68},{68... | collective-permute-start | bytes 393224 | tf_op jit(solution)/shard_map/ppermute | solution.py:190
  153.1 13.5 %all_to_all.26 = bf16[32,16,128]{2,1,0:T(8,128)(2,1)S(1)} all-to-all(bf16[32,16,128]{2,1,0:T(8,128)(2,1)S(1)} %bitcast.33), channel_id=1, replica_groups=mesh['yh'=2,'core'=2,'z'=8,'x'=4,'yl'=2] {'z','x'}, dimensions={0} | all-to-all | bytes 262144 | tf_op jit(solution)/shard_map/all_to_all | solution.py:194
  166.6 2.4 %collective-permute-start.21 = (f32[16,128]{1,0:T(8,128)S(1)}, f32[16,128]{1,0:T(8,128)S(1)}, u32[]{:S(2)}, u32[]{:S(2)}) collective-permute-start(f32[16,128]{1,0:T(8,128)S(1)} %convert_reduce_fusion), channel_id=1, source_target_pairs={{0,129},{1,0},{128,1},{129,128},{2,131},{3,2},{130,3},{131,130},{4... | collective-permute-start | bytes 24584 | tf_op jit(solution)/shard_map/ppermute | solution.py:186
  173.1 13.1 %all_to_all.27 = bf16[32,16,128]{2,1,0:T(8,128)(2,1)S(1)} all-to-all(bf16[32,16,128]{2,1,0:T(8,128)(2,1)S(1)} %broadcast_in_dim.2), channel_id=1, replica_groups=mesh['yh'=2,'core'=2,'z'=8,'x'=4,'yl'=2] {'z','x'}, dimensions={0} | all-to-all | bytes 262144 | tf_op jit(solution)/shard_map/all_to_all | solution.py:194
  186.2 4.1 %collective-permute-start.22 = (bf16[512,128]{1,0:T(8,128)(2,1)S(1)}, bf16[512,128]{1,0:T(8,128)(2,1)S(1)}, u32[]{:S(2)}, u32[]{:S(2)}) collective-permute-start(bf16[512,128]{1,0:T(8,128)(2,1)S(1)} %bitcast.32), channel_id=1, source_target_pairs={{0,64},{64,0},{1,65},{65,1},{2,66},{66,2},{3,67},{67,3},{4,68},{68... | collective-permute-start | bytes 393224 | tf_op jit(solution)/shard_map/ppermute | solution.py:190
  (110 shorter events, 38.3 us)
Async XLA Ops:
  34.8 20.3 %all-to-all-start.1 = ((bf16[32,8,1024]{2,1,0:T(8,128)(2,1)}), bf16[32,8,1024]{2,1,0:T(8,128)(2,1)S(1)}, u32[]{:S(2)}, u32[]{:S(2)}) async-start(bf16[32,8,1024]{2,1,0:T(8,128)(2,1)} %bitcast.4), calls=%async_computation.1 | async-start | bytes 1048576 | tf_op jit(solution)/shard_map/all_to_all | solution.py:194
  41.8 19.9 %collective-permute-start.1 = (bf16[2,64,1024]{2,1,0:T(8,128)(2,1)}, bf16[2,64,1024]{2,1,0:T(8,128)(2,1)}, u32[]{:S(2)}, u32[]{:S(2)}) collective-permute-start(bf16[2,64,1024]{2,1,0:T(8,128)(2,1)} %get-tuple-element.35), channel_id=1, source_target_pairs={{0,129},{1,0},{128,1},{129,128},{2,131},{3,2},{130,3},{131,130},{4... | collective-permute-start | bytes 786440 | tf_op jit(solution)/shard_map/ppermute | solution.py:186
  44.5 21.8 %collective-permute-start = (bf16[2,64,1024]{2,1,0:T(8,128)(2,1)}, bf16[2,64,1024]{2,1,0:T(8,128)(2,1)}, u32[]{:S(2)}, u32[]{:S(2)}) collective-permute-start(bf16[2,64,1024]{2,1,0:T(8,128)(2,1)} %get-tuple-element.35), channel_id=1, source_target_pairs={{0,1},{1,128},{128,129},{129,0},{2,3},{3,130},{130,131},{131,2},{4... | collective-permute-start | bytes 786440 | tf_op jit(solution)/shard_map/ppermute | solution.py:186
  57.3 10.8 %collective-permute-start.4 = (bf16[2,64,1024]{2,1,0:T(8,128)(2,1)S(1)}, bf16[2,64,1024]{2,1,0:T(8,128)(2,1)S(1)}, u32[]{:S(2)}, u32[]{:S(2)}) collective-permute-start(bf16[2,64,1024]{2,1,0:T(8,128)(2,1)S(1)} %get-tuple-element.38), channel_id=1, source_target_pairs={{0,129},{1,0},{128,1},{129,128},{2,131},{3,2},{130,3},{131,130},{4... | collective-permute-start | bytes 786440 | tf_op jit(solution)/shard_map/ppermute | solution.py:186
  60.1 19.4 %collective-permute-start.3 = (bf16[2,64,1024]{2,1,0:T(8,128)(2,1)S(1)}, bf16[2,64,1024]{2,1,0:T(8,128)(2,1)S(1)}, u32[]{:S(2)}, u32[]{:S(2)}) collective-permute-start(bf16[2,64,1024]{2,1,0:T(8,128)(2,1)S(1)} %get-tuple-element.38), channel_id=1, source_target_pairs={{0,1},{1,128},{128,129},{129,0},{2,3},{3,130},{130,131},{131,2},{4... | collective-permute-start | bytes 786440 | tf_op jit(solution)/shard_map/ppermute | solution.py:186
  60.1 21.9 %collective-permute-start.2 = (bf16[2,64,1024]{2,1,0:T(8,128)(2,1)}, bf16[2,64,1024]{2,1,0:T(8,128)(2,1)}, u32[]{:S(2)}, u32[]{:S(2)}) collective-permute-start(bf16[2,64,1024]{2,1,0:T(8,128)(2,1)} %copy-done.16), channel_id=1, source_target_pairs={{0,128},{1,129},{128,0},{129,1},{2,130},{3,131},{130,2},{131,3},{4... | collective-permute-start | bytes 786440 | tf_op jit(solution)/shard_map/ppermute | solution.py:186
  61.7 20.2 %collective-permute-start.6 = (bf16[2,64,1024]{2,1,0:T(8,128)(2,1)S(1)}, bf16[2,64,1024]{2,1,0:T(8,128)(2,1)S(1)}, u32[]{:S(2)}, u32[]{:S(2)}) collective-permute-start(bf16[2,64,1024]{2,1,0:T(8,128)(2,1)S(1)} %get-tuple-element.37.refs_0_), channel_id=1, source_target_pairs={{0,64},{64,0},{1,65},{65,1},{2,66},{66,2},{3,67},{67,3},{4,68},{68... | collective-permute-start | bytes 786440 | tf_op jit(solution)/shard_map/ppermute | solution.py:190
  66.3 16.8 %collective-permute-start.5 = (bf16[2,64,1024]{2,1,0:T(8,128)(2,1)S(1)}, bf16[2,64,1024]{2,1,0:T(8,128)(2,1)}, u32[]{:S(2)}, u32[]{:S(2)}) collective-permute-start(bf16[2,64,1024]{2,1,0:T(8,128)(2,1)S(1)} %get-tuple-element.37.refs_0_), channel_id=1, source_target_pairs={{0,128},{1,129},{128,0},{129,1},{2,130},{3,131},{130,2},{131,3},{4... | collective-permute-start | bytes 786440 | tf_op jit(solution)/shard_map/ppermute | solution.py:186
  68.1 15.1 %collective-permute-start.8 = (bf16[2,64,1024]{2,1,0:T(8,128)(2,1)S(1)}, bf16[2,64,1024]{2,1,0:T(8,128)(2,1)S(1)}, u32[]{:S(2)}, u32[]{:S(2)}) collective-permute-start(bf16[2,64,1024]{2,1,0:T(8,128)(2,1)S(1)} %collective-permute-done.4.refs_2_), channel_id=1, source_target_pairs={{0,64},{64,0},{1,65},{65,1},{2,66},{66,2},{3,67},{67,3},{4,68},{68... | collective-permute-start | bytes 786440 | tf_op jit(solution)/shard_map/ppermute | solution.py:190
  79.4 5.0 %collective-permute-start.7 = (bf16[2,64,1024]{2,1,0:T(8,128)(2,1)S(1)}, bf16[2,64,1024]{2,1,0:T(8,128)(2,1)S(1)}, u32[]{:S(2)}, u32[]{:S(2)}) collective-permute-start(bf16[2,64,1024]{2,1,0:T(8,128)(2,1)S(1)} %collective-permute-done.3.refs_1_), channel_id=1, source_target_pairs={{0,64},{64,0},{1,65},{65,1},{2,66},{66,2},{3,67},{67,3},{4,68},{68... | collective-permute-start | bytes 786440 | tf_op jit(solution)/shard_map/ppermute | solution.py:190
  81.9 14.7 %collective-permute-start.10 = (bf16[2,64,1024]{2,1,0:T(8,128)(2,1)}, bf16[2,64,1024]{2,1,0:T(8,128)(2,1)}, u32[]{:S(2)}, u32[]{:S(2)}) collective-permute-start(bf16[2,64,1024]{2,1,0:T(8,128)(2,1)} %copy-done.16), channel_id=1, source_target_pairs={{0,64},{64,0},{1,65},{65,1},{2,66},{66,2},{3,67},{67,3},{4,68},{68... | collective-permute-start | bytes 786440 | tf_op jit(solution)/shard_map/ppermute | solution.py:190
  82.7 14.0 %collective-permute-start.12 = (bf16[2,64,1024]{2,1,0:T(8,128)(2,1)}, bf16[2,64,1024]{2,1,0:T(8,128)(2,1)}, u32[]{:S(2)}, u32[]{:S(2)}) collective-permute-start(bf16[2,64,1024]{2,1,0:T(8,128)(2,1)} %collective-permute-done.1.refs_2_), channel_id=1, source_target_pairs={{0,64},{64,0},{1,65},{65,1},{2,66},{66,2},{3,67},{67,3},{4,68},{68... | collective-permute-start | bytes 786440 | tf_op jit(solution)/shard_map/ppermute | solution.py:190
  83.2 13.5 %collective-permute-start.11 = (bf16[2,64,1024]{2,1,0:T(8,128)(2,1)}, bf16[2,64,1024]{2,1,0:T(8,128)(2,1)}, u32[]{:S(2)}, u32[]{:S(2)}) collective-permute-start(bf16[2,64,1024]{2,1,0:T(8,128)(2,1)} %collective-permute-done.refs_1_), channel_id=1, source_target_pairs={{0,64},{64,0},{1,65},{65,1},{2,66},{66,2},{3,67},{67,3},{4,68},{68... | collective-permute-start | bytes 786440 | tf_op jit(solution)/shard_map/ppermute | solution.py:190
  83.9 12.8 %collective-permute-start.13 = (bf16[2,64,1024]{2,1,0:T(8,128)(2,1)}, bf16[2,64,1024]{2,1,0:T(8,128)(2,1)}, u32[]{:S(2)}, u32[]{:S(2)}) collective-permute-start(bf16[2,64,1024]{2,1,0:T(8,128)(2,1)} %collective-permute-done.2.refs_3_), channel_id=1, source_target_pairs={{0,64},{64,0},{1,65},{65,1},{2,66},{66,2},{3,67},{67,3},{4,68},{68... | collective-permute-start | bytes 786440 | tf_op jit(solution)/shard_map/ppermute | solution.py:190
  100.6 4.5 %collective-permute-start.14 = (bf16[4,2,64,1024]{3,2,1,0:T(8,128)(2,1)S(1)}, bf16[4,2,64,1024]{3,2,1,0:T(8,128)(2,1)S(1)}, u32[]{:S(2)}, u32[]{:S(2)}) collective-permute-start(bf16[4,2,64,1024]{3,2,1,0:T(8,128)(2,1)S(1)} %get-tuple-element.45), channel_id=1, source_target_pairs={{0,64},{64,0},{1,65},{65,1},{2,66},{66,2},{3,67},{67,3},{4,68},{68... | collective-permute-start | bytes 3145736 | tf_op jit(solution)/shard_map/ppermute | solution.py:190
  106.9 9.5 %collective-permute-start.17 = (bf16[2,64,1024]{2,1,0:T(8,128)(2,1)S(1)}, bf16[2,64,1024]{2,1,0:T(8,128)(2,1)S(1)}, u32[]{:S(2)}, u32[]{:S(2)}) collective-permute-start(bf16[2,64,1024]{2,1,0:T(8,128)(2,1)S(1)} %get-tuple-element.62), channel_id=1, source_target_pairs={{0,1},{1,128},{128,129},{129,0},{2,3},{3,130},{130,131},{131,2},{4... | collective-permute-start | bytes 786440 | tf_op jit(solution)/shard_map/ppermute | solution.py:186
  106.9 13.5 %collective-permute-start.16 = (bf16[2,64,1024]{2,1,0:T(8,128)(2,1)S(1)}, bf16[2,64,1024]{2,1,0:T(8,128)(2,1)S(1)}, u32[]{:S(2)}, u32[]{:S(2)}) collective-permute-start(bf16[2,64,1024]{2,1,0:T(8,128)(2,1)S(1)} %get-tuple-element.63), channel_id=1, source_target_pairs={{0,129},{1,0},{128,1},{129,128},{2,131},{3,2},{130,3},{131,130},{4... | collective-permute-start | bytes 786440 | tf_op jit(solution)/shard_map/ppermute | solution.py:186
  109.6 11.7 %collective-permute-start.15 = (bf16[2,64,1024]{2,1,0:T(8,128)(2,1)S(1)}, bf16[2,64,1024]{2,1,0:T(8,128)(2,1)S(1)}, u32[]{:S(2)}, u32[]{:S(2)}) collective-permute-start(bf16[2,64,1024]{2,1,0:T(8,128)(2,1)S(1)} %get-tuple-element.64), channel_id=1, source_target_pairs={{0,128},{1,129},{128,0},{129,1},{2,130},{3,131},{130,2},{131,3},{4... | collective-permute-start | bytes 786440 | tf_op jit(solution)/shard_map/ppermute | solution.py:186
  122.4 22.3 %all-to-all-start.2 = ((bf16[32,8,1024]{2,1,0:T(8,128)(2,1)}), bf16[32,8,1024]{2,1,0:T(8,128)(2,1)S(1)}, u32[]{:S(2)}, u32[]{:S(2)}) async-start(bf16[32,8,1024]{2,1,0:T(8,128)(2,1)} %bitcast.10), calls=%async_computation.2 | async-start | bytes 1048576 | tf_op jit(solution)/shard_map/all_to_all | solution.py:194
  148.5 4.5 %collective-permute-start.18 = (bf16[512,128]{1,0:T(8,128)(2,1)S(1)}, bf16[512,128]{1,0:T(8,128)(2,1)S(1)}, u32[]{:S(2)}, u32[]{:S(2)}) collective-permute-start(bf16[512,128]{1,0:T(8,128)(2,1)S(1)} %get-tuple-element.55), channel_id=1, source_target_pairs={{0,64},{64,0},{1,65},{65,1},{2,66},{66,2},{3,67},{67,3},{4,68},{68... | collective-permute-start | bytes 393224 | tf_op jit(solution)/shard_map/ppermute | solution.py:190
  166.6 6.4 %collective-permute-start.21 = (f32[16,128]{1,0:T(8,128)S(1)}, f32[16,128]{1,0:T(8,128)S(1)}, u32[]{:S(2)}, u32[]{:S(2)}) collective-permute-start(f32[16,128]{1,0:T(8,128)S(1)} %convert_reduce_fusion), channel_id=1, source_target_pairs={{0,129},{1,0},{128,1},{129,128},{2,131},{3,2},{130,3},{131,130},{4... | collective-permute-start | bytes 24584 | tf_op jit(solution)/shard_map/ppermute | solution.py:186
  169.0 4.0 %collective-permute-start.20 = (f32[16,128]{1,0:T(8,128)S(1)}, f32[16,128]{1,0:T(8,128)S(1)}, u32[]{:S(2)}, u32[]{:S(2)}) collective-permute-start(f32[16,128]{1,0:T(8,128)S(1)} %convert_reduce_fusion), channel_id=1, source_target_pairs={{0,1},{1,128},{128,129},{129,0},{2,3},{3,130},{130,131},{131,2},{4... | collective-permute-start | bytes 24584 | tf_op jit(solution)/shard_map/ppermute | solution.py:186
  169.0 4.0 %collective-permute-start.19 = (f32[16,128]{1,0:T(8,128)S(1)}, f32[16,128]{1,0:T(8,128)S(1)}, u32[]{:S(2)}, u32[]{:S(2)}) collective-permute-start(f32[16,128]{1,0:T(8,128)S(1)} %convert_reduce_fusion), channel_id=1, source_target_pairs={{0,128},{1,129},{128,0},{129,1},{2,130},{3,131},{130,2},{131,3},{4... | collective-permute-start | bytes 24584 | tf_op jit(solution)/shard_map/ppermute | solution.py:186
  186.2 5.1 %collective-permute-start.22 = (bf16[512,128]{1,0:T(8,128)(2,1)S(1)}, bf16[512,128]{1,0:T(8,128)(2,1)S(1)}, u32[]{:S(2)}, u32[]{:S(2)}) collective-permute-start(bf16[512,128]{1,0:T(8,128)(2,1)S(1)} %bitcast.32), channel_id=1, source_target_pairs={{0,64},{64,0},{1,65},{65,1},{2,66},{66,2},{3,67},{67,3},{4,68},{68... | collective-permute-start | bytes 393224 | tf_op jit(solution)/shard_map/ppermute | solution.py:190
  (31 other events, 232.0 us)
where the time goes:
time: 193 us; the launch traced here: 192 us
  blocking collectives  54.5 us (28%)
  starting transfers between devices  53 us (27%)
  waiting for transfers between devices  32.2 us (17%)
  Pallas kernels  20.3 us (11%)
  local copies, waits for them, and re-layouts  19.5 us (10%)
  matrix products  10.4 us (5%)
    all_to_all x3, blocking collectives, exchange(): return lax.all_to_all(value, ZX, split_axis=0, concat_axis=0, tiled=True)  54.5 us
    ppermute x11, starting transfers between devices, to_core(): return lax.ppermute(value, 'core', CORE_SWAP)  26.3 us
    all_to_all x2, waiting for transfers between devices, exchange(): return lax.all_to_all(value, ZX, split_axis=0, concat_axis=0, tiled=True)  21.7 us
    pallas_call x10, Pallas kernels, call(): pl.pallas_call(kernel, out_shape=out_shape, grid=grid, in_specs=in_specs,...  20.3 us
    unnamed x60, local copies, waits for them, and re-layouts  19.5 us
    ppermute x12, starting transfers between devices, to_y(): return lax.ppermute(value, Y, [(i, (i + step) % 4) for i in range(4)])  14.7 us
    all_to_all x2, starting transfers between devices, exchange(): return lax.all_to_all(value, ZX, split_axis=0, concat_axis=0, tiled=True)  12 us
    ppermute x12, waiting for transfers between devices, to_y(): return lax.ppermute(value, Y, [(i, (i + step) % 4) for i in range(4)])  8.55 us
  transfers between devices with their start and end apart: 25, of which 8 were waited for; matrix products, arithmetic and copies ran while one was open for 5% of the time, Pallas kernels for 5%

commit v1 on v0

--- a/solution.py
+++ b/solution.py
@@ -26,12 +26,16 @@
     return jnp.where(test, 1.0, 0.0).astype(bf16)
 
 
-def message_rows(shape, axis, yl, frames):
+def message_rows(shape, axis, yl, frames, arrays):
     row = lax.broadcasted_iota(jnp.int32, shape, axis)
+    experts = shape[axis] // (frames * arrays)
     frame = row & (frames - 1)
     rest = row // frames
-    expert = (rest // 4) * 4 + ((((rest // 2) & 1) ^ yl) * 2) + (rest & 1)
-    return frame * (shape[axis] // frames) + expert
+    pair = rest & 1
+    array = (rest // 2) & (arrays - 1)
+    rest = rest // (2 * arrays)
+    expert = (rest // 2) * 4 + ((rest & 1) ^ yl) * 2 + pair
+    return (array * frames + frame) * experts + expert
 
 
 def call(kernel, out_shape, *args, grid=(), in_specs=None, out_specs=None, vmem=16, flops=0, **kw):
@@ -62,52 +66,63 @@
 ANY = pl.BlockSpec(memory_space=pl.ANY)
 
 
-def to_message(place_ref, slots, out_ref):
-    rows = out_ref.shape[0]
-    yl = place_ref[0]
+def load(source, target, sems, i):
+    copy = pltpu.make_async_copy(source, target, sems.at[i])
+    copy.start()
+    return copy
+
+
+def softmax(logits, axis):
+    up = jnp.exp(logits - jnp.max(logits, axis=axis, keepdims=True))
+    return up / jnp.sum(up, axis=axis, keepdims=True)
+
+
+def prep_kernel(
+    place_ref, params_hbm, tokens_hbm, out_grad_hbm, message_ref, dispatch_ref, combine_ref,
+    params_ref, tokens_ref, out_grad_ref, sems,
+):
+    frames = tokens_ref.shape[0]
+    rows = message_ref.shape[0]
+    copies = [load(params_hbm, params_ref, sems, 2 * frames)]
+    copies += [load(tokens_hbm.at[f], tokens_ref.at[f], sems, f) for f in range(frames)]
+    copies += [load(out_grad_hbm.at[f], out_grad_ref.at[f], sems, frames + f) for f in range(frames)]
     order = one_hot(
-        message_rows((rows, rows), 0, yl, len(slots)) == lax.broadcasted_iota(jnp.int32, (rows, rows), 1)
-    )
-    out_ref[...] = dot(order, jnp.concatenate(slots, axis=0)).astype(bf16)
-
-
-def prep_kernel(place_ref, tokens_ref, params_ref, message_ref, dispatch_ref, combine_ref):
-    slots = []
-    for f in range(tokens_ref.shape[0]):
+        message_rows((rows, rows), 0, place_ref[0], frames, 2)
+        == lax.broadcasted_iota(jnp.int32, (rows, rows), 1)
+    )
+    copies[0].wait()
+    slots_in, slot_grad = [], []
+    for f in range(frames):
+        copies[1 + f].wait()
         tokens = tokens_ref[f]
         logits = dot(tokens, params_ref[...])
-        up = jnp.exp(logits - jnp.max(logits, axis=0, keepdims=True))
-        dispatch = up / jnp.sum(up, axis=0, keepdims=True)
+        dispatch = softmax(logits, 0)
+        combine = softmax(logits, 1)
         dispatch_ref[f] = dispatch
-        slots.append(dot(dispatch.astype(bf16), tokens, ((0,), (0,))).astype(bf16))
-        up = jnp.exp(logits - jnp.max(logits, axis=1, keepdims=True))
-        combine_ref[f] = up / jnp.sum(up, axis=1, keepdims=True)
-    to_message(place_ref, slots, message_ref)
-
-
-def grad_kernel(place_ref, combine_ref, out_grad_ref, message_ref):
-    slots = []
-    for f in range(out_grad_ref.shape[0]):
-        low = combine_ref[f].astype(bf16)
-        slots.append(dot(low, out_grad_ref[f], ((0,), (0,))).astype(bf16))
-    to_message(place_ref, slots, message_ref)
-
-
-def sort_order(rows, frames, axis):
+        combine_ref[f] = combine
+        slots_in.append(dot(dispatch.astype(bf16), tokens, ((0,), (0,))).astype(bf16))
+        copies[1 + frames + f].wait()
+        slot_grad.append(dot(combine.astype(bf16), out_grad_ref[f], ((0,), (0,))).astype(bf16))
+    message_ref[...] = dot(order, jnp.concatenate(slots_in + slot_grad, axis=0)).astype(bf16)
+
+
+def sort_order(rows, frames, arrays, axis):
     row = lax.broadcasted_iota(jnp.int32, (rows, rows), axis)
-    pair = row // (rows // 4)
-    rest = row - pair * (rows // 4)
-    return (rest // frames) * (4 * frames) + pair * frames + (rest & (frames - 1))
-
-
-def sort_kernel(frames, message_ref, own_ref, other_ref):
+    kinds = 4 * arrays
+    kind = row // (rows // kinds)
+    rest = row - kind * (rows // kinds)
+    return (rest // frames) * (kinds * frames) + kind * frames + (rest & (frames - 1))
+
+
+def sort_kernel(frames, message_ref, *out_refs):
     rows, depth = message_ref.shape
     order = one_hot(
-        sort_order(rows, frames, 0) == lax.broadcasted_iota(jnp.int32, (rows, rows), 1)
+        sort_order(rows, frames, 2, 0) == lax.broadcasted_iota(jnp.int32, (rows, rows), 1)
     )
     out = dot(order, message_ref[...]).astype(bf16)
-    own_ref[...] = out[: rows // 2].reshape(own_ref.shape)
-    other_ref[...] = out[rows // 2 :].reshape(other_ref.shape)
+    part = rows // len(out_refs)
+    for i, out_ref in enumerate(out_refs):
+        out_ref[...] = out[i * part : (i + 1) * part].reshape(out_ref.shape)
 
 
 def unsort_kernel(frames, own_ref, across_ref, back_ref, ahead_ref, message_ref):
@@ -119,29 +134,29 @@
 
     value = jnp.concatenate([total(own_ref, across_ref), total(back_ref, ahead_ref)], axis=0)
     order = one_hot(
-        sort_order(rows, frames, 1) == lax.broadcasted_iota(jnp.int32, (rows, rows), 0)
+        sort_order(rows, frames, 1, 1) == lax.broadcasted_iota(jnp.int32, (rows, rows), 0)
     )
     message_ref[...] = dot(order, value).astype(bf16)
 
 
 def hidden_kernel(*refs):
-    pieces, w_in_ref, rows_ref, hidden_ref = refs[:8], refs[8], refs[9], refs[10]
+    pieces, w_in_ref, rows_ref, active_ref, slope_ref = refs[:8], *refs[8:]
     rows = jnp.concatenate([piece[0] for piece in pieces], axis=0)
     rows_ref[0] = rows
-    hidden_ref[0] = dot(rows, w_in_ref[0])
-
-
-def expert_kernel(*refs):
-    pieces, hidden_ref, w_in_ref, w_out_ref = refs[:4], refs[4], refs[5], refs[6]
-    rows_ref, active_ref, pre_ref, partial_ref = refs[-4:]
-    rows = jnp.concatenate([piece[0] for piece in pieces], axis=0)
-    rows_ref[0] = rows
-    hidden = hidden_ref[0]
+    hidden = dot(rows, w_in_ref[0])
     cdf = 0.5 * (1.0 + lax.erf(hidden * inv_root_two))
     dens = jnp.exp(-0.5 * hidden * hidden) * inv_root_tau
     active_ref[0] = (hidden * cdf).astype(bf16)
+    slope_ref[0] = (cdf + hidden * dens).astype(slope_ref.dtype)
+
+
+def expert_kernel(*refs):
+    pieces, slope_ref, w_in_ref, w_out_ref = refs[:4], refs[4], refs[5], refs[6]
+    rows_ref, pre_ref, partial_ref = refs[-3:]
+    rows = jnp.concatenate([piece[0] for piece in pieces], axis=0)
+    rows_ref[0] = rows
     act_grad = dot(rows, w_out_ref[0], ((1,), (1,)))
-    pre = (act_grad * (cdf + hidden * dens)).astype(bf16)
+    pre = (act_grad * slope_ref[0].astype(f32)).astype(bf16)
     pre_ref[0] = pre
     partial = dot(pre, w_in_ref[0], ((1,), (1,)))
     partial_ref[...] = partial.astype(partial_ref.dtype).reshape(partial_ref.shape)
@@ -151,7 +166,7 @@
     rows, depth = message_ref.shape
     frames, experts = slots_ref.shape[:2]
     order = one_hot(
-        message_rows((rows, rows), 1, place_ref[0], frames)
+        message_rows((rows, rows), 1, place_ref[0], frames, 1)
         == lax.broadcasted_iota(jnp.int32, (rows, rows), 0)
     )
     slots = dot(order, message_ref[...]).astype(bf16)
@@ -194,25 +209,14 @@
     return lax.all_to_all(value, ZX, split_axis=0, concat_axis=0, tiled=True)
 
 
-def spread(message, groups, frames):
-    rows, depth = message.shape
-    message = exchange(message.reshape(groups, rows // groups, depth)).reshape(rows, depth)
-    half = shape((2, rows // 4, depth), bf16)
-    own, other = call(
-        functools.partial(sort_kernel, frames), (half, half), message, flops=2 * rows * rows * depth
-    )
-    near = [own, to_y(other, 1), to_y(other, -1), to_y(own, 2)]
-    return near, [to_core(piece) for piece in near]
-
-
 def sum_all(mine, theirs, groups, beside):
     half, cols = mine.shape
     core = lax.axis_index("core")
     mine = (mine + to_core(theirs).astype(f32)).astype(bf16)
     pieces = exchange(mine.reshape(groups, half // groups, cols))
+    pieces, beside = lax.optimization_barrier((pieces, beside))
     part = jnp.sum(pieces.astype(f32), axis=0)
     across, back, ahead = to_y(part, 2), to_y(part, 1), to_y(part, -1)
-    across, beside = lax.optimization_barrier((across, beside))
     total = ((part + across) + (back + ahead)).astype(bf16)
     mine = exchange(jnp.broadcast_to(total[None], (groups,) + total.shape)).reshape(half, cols)
     theirs = to_core(mine)
@@ -235,19 +239,20 @@
     message, dispatch, combine = call(
         prep_kernel,
         (
-            shape((rows, depth), bf16),
+            shape((2 * rows, depth), bf16),
             shape((frames, patch, experts), f32),
             shape((frames, patch, experts), f32),
         ),
-        place, tokens, slot_params,
-        in_specs=[SMEM, VMEM, VMEM], flops=2 * frame_flops + sort_flops,
-    )
-    near_in, far_in = spread(message, groups, frames)
-    message = call(
-        grad_kernel, shape((rows, depth), bf16), place, combine, out_grad,
-        in_specs=[SMEM, VMEM, VMEM], flops=frame_flops + sort_flops,
-    )
-    near_grad, far_grad = spread(message, groups, frames)
+        place, slot_params, tokens, out_grad,
+        in_specs=[SMEM, ANY, ANY, ANY], vmem=56, flops=3 * frame_flops + 4 * sort_flops,
+        scratch_shapes=[
+            pltpu.VMEM((depth, experts), bf16),
+            pltpu.VMEM((frames, patch, depth), bf16),
+            pltpu.VMEM((frames, patch, depth), bf16),
+            pltpu.SemaphoreType.DMA((2 * frames + 1,)),
+        ],
+    )
+    message = exchange(message.reshape(groups, 2 * rows // groups, depth)).reshape(2 * rows, depth)
 
     combine_grad = jnp.einsum(
         "fpd,fed->fpe", out_grad, slot_outputs, preferred_element_type=f32
@@ -255,25 +260,41 @@
     combine_part = combine * (
         combine_grad - jnp.sum(combine * combine_grad, axis=2, keepdims=True)
     )
+    message, combine_part = lax.optimization_barrier((message, combine_part))
+
+    own_in, own_grad, other_in, other_grad = call(
+        functools.partial(sort_kernel, frames), (shape((2, block, depth), bf16),) * 4, message,
+        flops=4 * sort_flops,
+    )
+    near_in = [own_in, to_y(other_in, 1), to_y(other_in, -1), to_y(own_in, 2)]
+    near_grad = [own_grad, to_y(other_grad, 1), to_y(other_grad, -1), to_y(own_grad, 2)]
+    far_in = [to_core(piece) for piece in near_in]
+    far_own = to_core(own_grad)
 
     piece = pl.BlockSpec((1, block, depth), lambda e: (e, 0, 0))
     w_in_spec = pl.BlockSpec((1, depth, hidden_size), lambda e: (e, 0, 0))
     w_out_spec = pl.BlockSpec((1, hidden_size, depth), lambda e: (e, 0, 0))
     matmul_flops = 2 * 2 * 8 * block * depth * hidden_size
-    slot_rows, hidden = call(
+    slot_rows, active, slope = call(
         hidden_kernel,
-        (shape((2, 8 * block, depth), bf16), shape((2, 8 * block, hidden_size), f32)),
+        (
+            shape((2, 8 * block, depth), bf16),
+            shape((2, 8 * block, hidden_size), bf16),
+            shape((2, 8 * block, hidden_size), bf16),
+        ),
         *near_in, *far_in, w_in,
         grid=(2,),
         in_specs=[piece] * 8 + [w_in_spec],
         out_specs=(
             pl.BlockSpec((1, 8 * block, depth), lambda e: (e, 0, 0)),
             pl.BlockSpec((1, 8 * block, hidden_size), lambda e: (e, 0, 0)),
+            pl.BlockSpec((1, 8 * block, hidden_size), lambda e: (e, 0, 0)),
         ),
-        vmem=20, flops=matmul_flops,
-    )
-
-    hidden, combine_part = lax.optimization_barrier((hidden, combine_part))
+        vmem=24, flops=matmul_flops,
+    )
+    slope, *arrived = lax.optimization_barrier((slope, *near_grad[1:]))
+    near_grad = [own_grad, *arrived]
+    far_grad = [far_own] + [to_core(piece) for piece in arrived]
 
     def expert_half(half, pieces, filled):
         rows_spec = pl.BlockSpec((1, 4 * block, depth), lambda e: (e, half, 0))
@@ -283,15 +304,13 @@
             (
                 shape((2, 8 * block, depth), bf16),
                 shape((2, 8 * block, hidden_size), bf16),
-                shape((2, 8 * block, hidden_size), bf16),
                 shape((4, 2, block, depth), bf16 if half else f32),
             ),
-            *pieces, hidden, w_in, w_out, *filled,
+            *pieces, slope, w_in, w_out, *filled,
             grid=(2,),
             in_specs=[piece] * 4 + [hidden_spec, w_in_spec, w_out_spec] + [ANY] * len(filled),
             out_specs=(
                 rows_spec,
-                hidden_spec,
                 hidden_spec,
                 pl.BlockSpec((4, 1, block, depth), lambda e: (0, e, 0, 0)),
             ),
@@ -301,7 +320,7 @@
 
     *filled, far = expert_half(1, far_grad, ())
     far = to_core(far)
-    grad_rows, active, pre_grad, near = expert_half(0, near_grad, filled)
+    grad_rows, pre_grad, near = expert_half(0, near_grad, filled)
 
     def summed(i):
         return (near[i] + far[i].astype(f32)).astype(bf16)

time: 193 us -> 177 us (0.917)
  blocking collectives: 54.5 us -> 13.1 us
  waiting for transfers between devices: 32.2 us -> 63.9 us
  local copies, waits for them, and re-layouts: 19.5 us -> 6.16 us
  starting transfers between devices: 53 us -> 59.8 us
    all_to_all x3 -> x1, blocking collectives: 54.5 us -> 13.1 us  [exchange(): return lax.all_to_all(value, ZX, split_axis=0, concat_axis=0, tiled=True)]
    all_to_all x2 -> x3, waiting for transfers between devices: 21.7 us -> 40.3 us  [exchange(): return lax.all_to_all(value, ZX, split_axis=0, concat_axis=0, tiled=True)]
    unnamed x60 -> x22, local copies, waits for them, and re-layouts: 19.5 us -> 6.13 us
    ppermute x12, waiting for transfers between devices: 8.55 us -> 20.2 us  [to_y(): return lax.ppermute(value, Y, [(i, (i + step) % 4) for i in range(4)])]
    all_to_all x2 -> x3, starting transfers between devices: 12 us -> 22.5 us  [exchange(): return lax.all_to_all(value, ZX, split_axis=0, concat_axis=0, tiled=True)]
    ppermute x11, starting transfers between devices: 26.3 us -> 24.3 us  [to_core(): return lax.ppermute(value, 'core', CORE_SWAP)]
    pallas_call x10 -> x8, Pallas kernels: 20.3 us -> 19.5 us  [call(): pl.pallas_call(kernel, out_shape=out_shape, grid=grid, in_specs=in_specs,...]
  transfers between devices with their start and end apart: 25 -> 26, of which waited for: 8 -> 13; matrix products, arithmetic and copies ran while one was open for 5% -> 6% of each run, Pallas kernels for 5% -> 4%
where the time goes in v1:
time: 177 us; the launch traced here: 176 us
  waiting for transfers between devices  63.9 us (36%)
  starting transfers between devices  59.8 us (34%)
  Pallas kernels  19.5 us (11%)
  blocking collectives  13.1 us (7%)
  matrix products  10.3 us (6%)
  local copies, waits for them, and re-layouts  6.16 us (3%)
  other arithmetic  2.59 us (1%)
    all_to_all x3, waiting for transfers between devices, exchange(): return lax.all_to_all(value, ZX, split_axis=0, concat_axis=0, tiled=True)  40.3 us
    ppermute x11, starting transfers between devices, to_core(): return lax.ppermute(value, 'core', CORE_SWAP)  24.3 us
    all_to_all x3, starting transfers between devices, exchange(): return lax.all_to_all(value, ZX, split_axis=0, concat_axis=0, tiled=True)  22.5 us
    ppermute x12, waiting for transfers between devices, to_y(): return lax.ppermute(value, Y, [(i, (i + step) % 4) for i in range(4)])  20.2 us
    pallas_call x8, Pallas kernels, call(): pl.pallas_call(kernel, out_shape=out_shape, grid=grid, in_specs=in_specs,...  19.5 us
    all_to_all x1, blocking collectives, exchange(): return lax.all_to_all(value, ZX, split_axis=0, concat_axis=0, tiled=True)  13.1 us
    ppermute x12, starting transfers between devices, to_y(): return lax.ppermute(value, Y, [(i, (i + step) % 4) for i in range(4)])  12.9 us
    unnamed x22, local copies, waits for them, and re-layouts  6.13 us
  transfers between devices with their start and end apart: 26, of which 13 were waited for; matrix products, arithmetic and copies ran while one was open for 6% of the time, Pallas kernels for 4%

profile of v1, /device:TPU:1, one launch (start us, length us, event | category | flops | bytes accessed | tf_op | source)
XLA Modules:
  0.0 176.1 jit_solution(8136835938930152125)
XLA Ops:
  1.3 5.1 %shard_map.93 = (bf16[512,1024]{1,0:T(8,128)(2,1)}, f32[2,256,128]{2,1,0:T(8,128)}, f32[2,256,128]{2,1,0:T(8,128)}) custom-call(s32[2]{0:T(128)} %pad_add_fusion.place_ref, bf16[1024,128]{1,0:T(8,128)(2,1)} %params_ref.1, bf16[2,256,1024]{2,1,0:T(8,128)(2,1)} %tokens_ref.1, bf16[2,256,1024]{2,1,0:T(8,128)(2,1)} %out_grad_hbm.1), custom_call_target="tpu_custom_call" | custom-call | flops 939524096 | bytes 3932168 | tf_op jit(solution)/shard_map/pallas_call | solution.py:48
  6.4 12.0 %all-to-all-start = ((bf16[32,16,1024]{2,1,0:T(8,128)(2,1)}), bf16[32,16,1024]{2,1,0:T(8,128)(2,1)}, u32[]{:S(2)}, u32[]{:S(2)}) async-start(bf16[32,16,1024]{2,1,0:T(8,128)(2,1)} %bitcast.27), calls=%async_computation | async-start | bytes 2097152 | tf_op jit(solution)/shard_map/all_to_all | solution.py:209
  18.4 2.6 %fusion.2.part_ref = f32[2,256,128]{2,1,0:T(8,128)S(1)} fusion(f32[2,256,128]{2,1,0:T(8,128)} %get-tuple-element.37, bf16[2,256,1024]{2,1,0:T(8,128)(2,1)} %out_grad_hbm.1, bf16[2,128,1024]{2,1,0:T(8,128)(2,1)S(1)} %copy-done), kind=kOutput, calls=%fused_computation.4 | convolution fusion | flops 268632704 | bytes 2097152 | tf_op jit(solution)/shard_map/sub | solution.py:261
  21.0 23.6 %all-to-all-done = bf16[32,16,1024]{2,1,0:T(8,128)(2,1)} async-done(((bf16[32,16,1024]{2,1,0:T(8,128)(2,1)}), bf16[32,16,1024]{2,1,0:T(8,128)(2,1)}, u32[]{:S(2)}, u32[]{:S(2)}) %all-to-all-start) | async-done | bytes 1048608 | tf_op jit(solution)/shard_map/all_to_all | solution.py:209
  46.7 2.8 %collective-permute-start.1 = (bf16[2,64,1024]{2,1,0:T(8,128)(2,1)S(1)}, bf16[2,64,1024]{2,1,0:T(8,128)(2,1)S(1)}, u32[]{:S(2)}, u32[]{:S(2)}) collective-permute-start(bf16[2,64,1024]{2,1,0:T(8,128)(2,1)S(1)} %get-tuple-element.41), channel_id=1, source_target_pairs={{0,129},{1,0},{128,1},{129,128},{2,131},{3,2},{130,3},{131,130},{4... | collective-permute-start | bytes 786440 | tf_op jit(solution)/shard_map/ppermute | solution.py:201
  51.1 3.7 %collective-permute-start.3 = (bf16[2,64,1024]{2,1,0:T(8,128)(2,1)S(1)}, bf16[2,64,1024]{2,1,0:T(8,128)(2,1)S(1)}, u32[]{:S(2)}, u32[]{:S(2)}) collective-permute-start(bf16[2,64,1024]{2,1,0:T(8,128)(2,1)S(1)} %get-tuple-element.40.refs_0_), channel_id=1, source_target_pairs={{0,64},{64,0},{1,65},{65,1},{2,66},{66,2},{3,67},{67,3},{4,68},{68... | collective-permute-start | bytes 786440 | tf_op jit(solution)/shard_map/ppermute | solution.py:205
  54.8 7.2 %collective-permute-start.5 = (bf16[2,64,1024]{2,1,0:T(8,128)(2,1)S(1)}, bf16[2,64,1024]{2,1,0:T(8,128)(2,1)S(1)}, u32[]{:S(2)}, u32[]{:S(2)}) collective-permute-start(bf16[2,64,1024]{2,1,0:T(8,128)(2,1)S(1)} %collective-permute-done.1.refs_2_), channel_id=1, source_target_pairs={{0,64},{64,0},{1,65},{65,1},{2,66},{66,2},{3,67},{67,3},{4,68},{68... | collective-permute-start | bytes 786440 | tf_op jit(solution)/shard_map/ppermute | solution.py:205
  62.0 3.1 %collective-permute-start.4 = (bf16[2,64,1024]{2,1,0:T(8,128)(2,1)S(1)}, bf16[2,64,1024]{2,1,0:T(8,128)(2,1)S(1)}, u32[]{:S(2)}, u32[]{:S(2)}) collective-permute-start(bf16[2,64,1024]{2,1,0:T(8,128)(2,1)S(1)} %collective-permute-done.refs_1_), channel_id=1, source_target_pairs={{0,64},{64,0},{1,65},{65,1},{2,66},{66,2},{3,67},{67,3},{4,68},{68... | collective-permute-start | bytes 786440 | tf_op jit(solution)/shard_map/ppermute | solution.py:205
  67.8 2.5 %shard_map.95 = (bf16[2,512,1024]{2,1,0:T(8,128)(2,1)S(1)}, bf16[2,512,640]{2,1,0:T(8,128)(2,1)S(1)}, bf16[2,512,640]{2,1,0:T(8,128)(2,1)S(1)}) custom-call(bf16[2,64,1024]{2,1,0:T(8,128)(2,1)S(1)} %get-tuple-element.40.refs_0_, bf16[2,64,1024]{2,1,0:T(8,128)(2,1)S(1)} %collective-permute-done.refs_1_, ...), custom_call_target="tpu_custom_call" | custom-call | flops 1342177280 | bytes 9437184 | tf_op jit(solution)/shard_map/pallas_call | solution.py:48
  72.4 7.9 %collective-permute-done.7.refs_1_ = bf16[2,64,1024]{2,1,0:T(8,128)(2,1)S(1)} collective-permute-done((bf16[2,64,1024]{2,1,0:T(8,128)(2,1)S(1)}, bf16[2,64,1024]{2,1,0:T(8,128)(2,1)S(1)}, u32[]{:S(2)}, u32[]{:S(2)}) %collective-permute-start.7) | collective-permute-done | bytes 262176 | tf_op jit(solution)/shard_map/ppermute | solution.py:201
  83.4 2.7 %shard_map.96 = (bf16[2,512,1024]{2,1,0:T(8,128)(2,1)S(1)}, bf16[2,512,640]{2,1,0:T(8,128)(2,1)S(1)}, bf16[4,2,64,1024]{3,2,1,0:T(8,128)(2,1)S(1)}) custom-call(bf16[2,64,1024]{2,1,0:T(8,128)(2,1)S(1)} %collective-permute-done.10.refs_0_, bf16[2,64,1024]{2,1,0:T(8,128)(2,1)S(1)} %collective-permute-done.11.refs_1_, ...), custom_call_target="tpu_custom_call" | custom-call | flops 1342177280 | bytes 12058624 | tf_op jit(solution)/shard_map/pallas_call | solution.py:48
  86.6 2.8 %shard_map.97 = (bf16[2,512,1024]{2,1,0:T(8,128)(2,1)S(1)}, bf16[2,512,640]{2,1,0:T(8,128)(2,1)S(1)}, f32[4,2,64,1024]{3,2,1,0:T(8,128)S(1)}) custom-call(bf16[2,64,1024]{2,1,0:T(8,128)(2,1)S(1)} %get-tuple-element.39.refs_0_, bf16[2,64,1024]{2,1,0:T(8,128)(2,1)S(1)} %collective-permute-done.7.refs_1_, ...), custom_call_target="tpu_custom_call", output_to_operand_aliasing={{0}: (7, {}), {1}: (8, {})} | custom-call | flops 1342177280 | bytes 16515072 | tf_op jit(solution)/shard_map/pallas_call | solution.py:48
  90.6 2.7 %collective-permute-start.16 = (bf16[2,64,1024]{2,1,0:T(8,128)(2,1)S(1)}, bf16[2,64,1024]{2,1,0:T(8,128)(2,1)S(1)}, u32[]{:S(2)}, u32[]{:S(2)}) collective-permute-start(bf16[2,64,1024]{2,1,0:T(8,128)(2,1)S(1)} %get-tuple-element.69), channel_id=1, source_target_pairs={{0,129},{1,0},{128,1},{129,128},{2,131},{3,2},{130,3},{131,130},{4... | collective-permute-start | bytes 786440 | tf_op jit(solution)/shard_map/ppermute | solution.py:201
  93.3 3.3 %convolution_convert_fusion.1 = bf16[2,1024,640]{2,1,0:T(8,128)(2,1)} fusion(bf16[2,512,1024]{2,1,0:T(8,128)(2,1)S(1)} %get-tuple-element.52, bf16[2,512,640]{2,1,0:T(8,128)(2,1)S(1)} %get-tuple-element.53), kind=kOutput, calls=%fused_computation.2 | convolution fusion | flops 1343488000 | bytes 6029312 | tf_op jit(solution)/shard_map/erd,erh->edh/dot_general | solution.py:333
  96.7 8.6 %collective-permute-done.17.ahead_ref = bf16[2,64,1024]{2,1,0:T(8,128)(2,1)S(1)} collective-permute-done((bf16[2,64,1024]{2,1,0:T(8,128)(2,1)S(1)}, bf16[2,64,1024]{2,1,0:T(8,128)(2,1)S(1)}, u32[]{:S(2)}, u32[]{:S(2)}) %collective-permute-start.17) | collective-permute-done | bytes 262176 | tf_op jit(solution)/shard_map/ppermute | solution.py:201
  106.4 6.0 %all-to-all-start.1 = ((bf16[32,8,1024]{2,1,0:T(8,128)(2,1)}), bf16[32,8,1024]{2,1,0:T(8,128)(2,1)S(1)}, u32[]{:S(2)}, u32[]{:S(2)}) async-start(bf16[32,8,1024]{2,1,0:T(8,128)(2,1)} %bitcast.8), calls=%async_computation.1 | async-start | bytes 1048576 | tf_op jit(solution)/shard_map/all_to_all | solution.py:209
  112.4 4.4 %convolution_convert_fusion = bf16[2,640,1024]{2,1,0:T(8,128)(2,1)} fusion(bf16[2,512,640]{2,1,0:T(8,128)(2,1)} %copy-done.10, bf16[2,512,1024]{2,1,0:T(8,128)(2,1)S(1)} %copy-done.4), kind=kOutput, calls=%fused_computation.1 | convolution fusion | flops 1343488000 | bytes 6029312 | tf_op jit(solution)/shard_map/erh,erd->ehd/dot_general | solution.py:330
  116.8 11.0 %all-to-all-done.1 = bf16[32,8,1024]{2,1,0:T(8,128)(2,1)S(1)} async-done(((bf16[32,8,1024]{2,1,0:T(8,128)(2,1)}), bf16[32,8,1024]{2,1,0:T(8,128)(2,1)S(1)}, u32[]{:S(2)}, u32[]{:S(2)}) %all-to-all-start.1) | async-done | bytes 524320 | tf_op jit(solution)/shard_map/all_to_all | solution.py:209
  131.7 3.5 %collective-permute-start.18 = (bf16[512,128]{1,0:T(8,128)(2,1)S(1)}, bf16[512,128]{1,0:T(8,128)(2,1)S(1)}, u32[]{:S(2)}, u32[]{:S(2)}) collective-permute-start(bf16[512,128]{1,0:T(8,128)(2,1)S(1)} %get-tuple-element.61), channel_id=1, source_target_pairs={{0,64},{64,0},{1,65},{65,1},{2,66},{66,2},{3,67},{67,3},{4,68},{68... | collective-permute-start | bytes 393224 | tf_op jit(solution)/shard_map/ppermute | solution.py:205
  136.8 4.5 %all-to-all-start.2 = ((bf16[32,16,128]{2,1,0:T(8,128)(2,1)}), bf16[32,16,128]{2,1,0:T(8,128)(2,1)S(1)}, u32[]{:S(2)}, u32[]{:S(2)}) async-start(bf16[32,16,128]{2,1,0:T(8,128)(2,1)} %bitcast.10), calls=%async_computation.2 | async-start | bytes 262144 | tf_op jit(solution)/shard_map/all_to_all | solution.py:209
  144.7 5.8 %all-to-all-done.2 = bf16[32,16,128]{2,1,0:T(8,128)(2,1)S(1)} async-done(((bf16[32,16,128]{2,1,0:T(8,128)(2,1)}), bf16[32,16,128]{2,1,0:T(8,128)(2,1)S(1)}, u32[]{:S(2)}, u32[]{:S(2)}) %all-to-all-start.2) | async-done | bytes 131104 | tf_op jit(solution)/shard_map/all_to_all | solution.py:209
  150.5 2.4 %collective-permute-start.21 = (f32[16,128]{1,0:T(8,128)S(1)}, f32[16,128]{1,0:T(8,128)S(1)}, u32[]{:S(2)}, u32[]{:S(2)}) collective-permute-start(f32[16,128]{1,0:T(8,128)S(1)} %convert_reduce_fusion), channel_id=1, source_target_pairs={{0,129},{1,0},{128,1},{129,128},{2,131},{3,2},{130,3},{131,130},{4... | collective-permute-start | bytes 24584 | tf_op jit(solution)/shard_map/ppermute | solution.py:201
  157.0 13.1 %all_to_all.20 = bf16[32,16,128]{2,1,0:T(8,128)(2,1)S(1)} all-to-all(bf16[32,16,128]{2,1,0:T(8,128)(2,1)S(1)} %broadcast_in_dim.2), channel_id=1, replica_groups=mesh['yh'=2,'core'=2,'z'=8,'x'=4,'yl'=2] {'z','x'}, dimensions={0} | all-to-all | bytes 262144 | tf_op jit(solution)/shard_map/all_to_all | solution.py:209
  170.1 4.1 %collective-permute-start.22 = (bf16[512,128]{1,0:T(8,128)(2,1)S(1)}, bf16[512,128]{1,0:T(8,128)(2,1)S(1)}, u32[]{:S(2)}, u32[]{:S(2)}) collective-permute-start(bf16[512,128]{1,0:T(8,128)(2,1)S(1)} %bitcast.28), channel_id=1, source_target_pairs={{0,64},{64,0},{1,65},{65,1},{2,66},{66,2},{3,67},{67,3},{4,68},{68... | collective-permute-start | bytes 393224 | tf_op jit(solution)/shard_map/ppermute | solution.py:205
  (70 shorter events, 30.0 us)
Async XLA Ops:
  6.4 38.2 %all-to-all-start = ((bf16[32,16,1024]{2,1,0:T(8,128)(2,1)}), bf16[32,16,1024]{2,1,0:T(8,128)(2,1)}, u32[]{:S(2)}, u32[]{:S(2)}) async-start(bf16[32,16,1024]{2,1,0:T(8,128)(2,1)} %bitcast.27), calls=%async_computation | async-start | bytes 2097152 | tf_op jit(solution)/shard_map/all_to_all | solution.py:209
  46.7 8.1 %collective-permute-start.1 = (bf16[2,64,1024]{2,1,0:T(8,128)(2,1)S(1)}, bf16[2,64,1024]{2,1,0:T(8,128)(2,1)S(1)}, u32[]{:S(2)}, u32[]{:S(2)}) collective-permute-start(bf16[2,64,1024]{2,1,0:T(8,128)(2,1)S(1)} %get-tuple-element.41), channel_id=1, source_target_pairs={{0,129},{1,0},{128,1},{129,128},{2,131},{3,2},{130,3},{131,130},{4... | collective-permute-start | bytes 786440 | tf_op jit(solution)/shard_map/ppermute | solution.py:201
  49.5 12.5 %collective-permute-start = (bf16[2,64,1024]{2,1,0:T(8,128)(2,1)S(1)}, bf16[2,64,1024]{2,1,0:T(8,128)(2,1)S(1)}, u32[]{:S(2)}, u32[]{:S(2)}) collective-permute-start(bf16[2,64,1024]{2,1,0:T(8,128)(2,1)S(1)} %get-tuple-element.41), channel_id=1, source_target_pairs={{0,1},{1,128},{128,129},{129,0},{2,3},{3,130},{130,131},{131,2},{4... | collective-permute-start | bytes 786440 | tf_op jit(solution)/shard_map/ppermute | solution.py:201
  49.5 15.6 %collective-permute-start.2 = (bf16[2,64,1024]{2,1,0:T(8,128)(2,1)S(1)}, bf16[2,64,1024]{2,1,0:T(8,128)(2,1)S(1)}, u32[]{:S(2)}, u32[]{:S(2)}) collective-permute-start(bf16[2,64,1024]{2,1,0:T(8,128)(2,1)S(1)} %get-tuple-element.40.refs_0_), channel_id=1, source_target_pairs={{0,128},{1,129},{128,0},{129,1},{2,130},{3,131},{130,2},{131,3},{4... | collective-permute-start | bytes 786440 | tf_op jit(solution)/shard_map/ppermute | solution.py:201
  51.1 14.8 %collective-permute-start.3 = (bf16[2,64,1024]{2,1,0:T(8,128)(2,1)S(1)}, bf16[2,64,1024]{2,1,0:T(8,128)(2,1)S(1)}, u32[]{:S(2)}, u32[]{:S(2)}) collective-permute-start(bf16[2,64,1024]{2,1,0:T(8,128)(2,1)S(1)} %get-tuple-element.40.refs_0_), channel_id=1, source_target_pairs={{0,64},{64,0},{1,65},{65,1},{2,66},{66,2},{3,67},{67,3},{4,68},{68... | collective-permute-start | bytes 786440 | tf_op jit(solution)/shard_map/ppermute | solution.py:205
  54.8 11.7 %collective-permute-start.5 = (bf16[2,64,1024]{2,1,0:T(8,128)(2,1)S(1)}, bf16[2,64,1024]{2,1,0:T(8,128)(2,1)S(1)}, u32[]{:S(2)}, u32[]{:S(2)}) collective-permute-start(bf16[2,64,1024]{2,1,0:T(8,128)(2,1)S(1)} %collective-permute-done.1.refs_2_), channel_id=1, source_target_pairs={{0,64},{64,0},{1,65},{65,1},{2,66},{66,2},{3,67},{67,3},{4,68},{68... | collective-permute-start | bytes 786440 | tf_op jit(solution)/shard_map/ppermute | solution.py:205
  62.0 5.2 %collective-permute-start.4 = (bf16[2,64,1024]{2,1,0:T(8,128)(2,1)S(1)}, bf16[2,64,1024]{2,1,0:T(8,128)(2,1)S(1)}, u32[]{:S(2)}, u32[]{:S(2)}) collective-permute-start(bf16[2,64,1024]{2,1,0:T(8,128)(2,1)S(1)} %collective-permute-done.refs_1_), channel_id=1, source_target_pairs={{0,64},{64,0},{1,65},{65,1},{2,66},{66,2},{3,67},{67,3},{4,68},{68... | collective-permute-start | bytes 786440 | tf_op jit(solution)/shard_map/ppermute | solution.py:205
  65.0 2.7 %collective-permute-start.6 = (bf16[2,64,1024]{2,1,0:T(8,128)(2,1)S(1)}, bf16[2,64,1024]{2,1,0:T(8,128)(2,1)S(1)}, u32[]{:S(2)}, u32[]{:S(2)}) collective-permute-start(bf16[2,64,1024]{2,1,0:T(8,128)(2,1)S(1)} %collective-permute-done.2.refs_3_), channel_id=1, source_target_pairs={{0,64},{64,0},{1,65},{65,1},{2,66},{66,2},{3,67},{67,3},{4,68},{68... | collective-permute-start | bytes 786440 | tf_op jit(solution)/shard_map/ppermute | solution.py:205
  65.0 7.4 %collective-permute-start.8 = (bf16[2,64,1024]{2,1,0:T(8,128)(2,1)S(1)}, bf16[2,64,1024]{2,1,0:T(8,128)(2,1)S(1)}, u32[]{:S(2)}, u32[]{:S(2)}) collective-permute-start(bf16[2,64,1024]{2,1,0:T(8,128)(2,1)S(1)} %get-tuple-element.43), channel_id=1, source_target_pairs={{0,129},{1,0},{128,1},{129,128},{2,131},{3,2},{130,3},{131,130},{4... | collective-permute-start | bytes 786440 | tf_op jit(solution)/shard_map/ppermute | solution.py:201
  65.9 14.4 %collective-permute-start.7 = (bf16[2,64,1024]{2,1,0:T(8,128)(2,1)S(1)}, bf16[2,64,1024]{2,1,0:T(8,128)(2,1)S(1)}, u32[]{:S(2)}, u32[]{:S(2)}) collective-permute-start(bf16[2,64,1024]{2,1,0:T(8,128)(2,1)S(1)} %get-tuple-element.43), channel_id=1, source_target_pairs={{0,1},{1,128},{128,129},{129,0},{2,3},{3,130},{130,131},{131,2},{4... | collective-permute-start | bytes 786440 | tf_op jit(solution)/shard_map/ppermute | solution.py:201
  66.5 13.8 %collective-permute-start.9 = (bf16[2,64,1024]{2,1,0:T(8,128)(2,1)S(1)}, bf16[2,64,1024]{2,1,0:T(8,128)(2,1)S(1)}, u32[]{:S(2)}, u32[]{:S(2)}) collective-permute-start(bf16[2,64,1024]{2,1,0:T(8,128)(2,1)S(1)} %get-tuple-element.39.refs_0_), channel_id=1, source_target_pairs={{0,128},{1,129},{128,0},{129,1},{2,130},{3,131},{130,2},{131,3},{4... | collective-permute-start | bytes 786440 | tf_op jit(solution)/shard_map/ppermute | solution.py:201
  67.1 14.9 %collective-permute-start.10 = (bf16[2,64,1024]{2,1,0:T(8,128)(2,1)S(1)}, bf16[2,64,1024]{2,1,0:T(8,128)(2,1)S(1)}, u32[]{:S(2)}, u32[]{:S(2)}) collective-permute-start(bf16[2,64,1024]{2,1,0:T(8,128)(2,1)S(1)} %get-tuple-element.39.refs_0_), channel_id=1, source_target_pairs={{0,64},{64,0},{1,65},{65,1},{2,66},{66,2},{3,67},{67,3},{4,68},{68... | collective-permute-start | bytes 786440 | tf_op jit(solution)/shard_map/ppermute | solution.py:205
  80.3 2.3 %collective-permute-start.11 = (bf16[2,64,1024]{2,1,0:T(8,128)(2,1)S(1)}, bf16[2,64,1024]{2,1,0:T(8,128)(2,1)S(1)}, u32[]{:S(2)}, u32[]{:S(2)}) collective-permute-start(bf16[2,64,1024]{2,1,0:T(8,128)(2,1)S(1)} %collective-permute-done.7.refs_1_), channel_id=1, source_target_pairs={{0,64},{64,0},{1,65},{65,1},{2,66},{66,2},{3,67},{67,3},{4,68},{68... | collective-permute-start | bytes 786440 | tf_op jit(solution)/shard_map/ppermute | solution.py:205
  86.1 3.2 %collective-permute-start.14 = (bf16[4,2,64,1024]{3,2,1,0:T(8,128)(2,1)S(1)}, bf16[4,2,64,1024]{3,2,1,0:T(8,128)(2,1)S(1)}, u32[]{:S(2)}, u32[]{:S(2)}) collective-permute-start(bf16[4,2,64,1024]{3,2,1,0:T(8,128)(2,1)S(1)} %get-tuple-element.51), channel_id=1, source_target_pairs={{0,64},{64,0},{1,65},{65,1},{2,66},{66,2},{3,67},{67,3},{4,68},{68... | collective-permute-start | bytes 3145736 | tf_op jit(solution)/shard_map/ppermute | solution.py:205
  90.6 14.6 %collective-permute-start.17 = (bf16[2,64,1024]{2,1,0:T(8,128)(2,1)S(1)}, bf16[2,64,1024]{2,1,0:T(8,128)(2,1)S(1)}, u32[]{:S(2)}, u32[]{:S(2)}) collective-permute-start(bf16[2,64,1024]{2,1,0:T(8,128)(2,1)S(1)} %get-tuple-element.68), channel_id=1, source_target_pairs={{0,1},{1,128},{128,129},{129,0},{2,3},{3,130},{130,131},{131,2},{4... | collective-permute-start | bytes 786440 | tf_op jit(solution)/shard_map/ppermute | solution.py:201
  90.6 14.6 %collective-permute-start.16 = (bf16[2,64,1024]{2,1,0:T(8,128)(2,1)S(1)}, bf16[2,64,1024]{2,1,0:T(8,128)(2,1)S(1)}, u32[]{:S(2)}, u32[]{:S(2)}) collective-permute-start(bf16[2,64,1024]{2,1,0:T(8,128)(2,1)S(1)} %get-tuple-element.69), channel_id=1, source_target_pairs={{0,129},{1,0},{128,1},{129,128},{2,131},{3,2},{130,3},{131,130},{4... | collective-permute-start | bytes 786440 | tf_op jit(solution)/shard_map/ppermute | solution.py:201
  93.3 11.9 %collective-permute-start.15 = (bf16[2,64,1024]{2,1,0:T(8,128)(2,1)S(1)}, bf16[2,64,1024]{2,1,0:T(8,128)(2,1)S(1)}, u32[]{:S(2)}, u32[]{:S(2)}) collective-permute-start(bf16[2,64,1024]{2,1,0:T(8,128)(2,1)S(1)} %get-tuple-element.70), channel_id=1, source_target_pairs={{0,128},{1,129},{128,0},{129,1},{2,130},{3,131},{130,2},{131,3},{4... | collective-permute-start | bytes 786440 | tf_op jit(solution)/shard_map/ppermute | solution.py:201
  106.4 21.4 %all-to-all-start.1 = ((bf16[32,8,1024]{2,1,0:T(8,128)(2,1)}), bf16[32,8,1024]{2,1,0:T(8,128)(2,1)S(1)}, u32[]{:S(2)}, u32[]{:S(2)}) async-start(bf16[32,8,1024]{2,1,0:T(8,128)(2,1)} %bitcast.8), calls=%async_computation.1 | async-start | bytes 1048576 | tf_op jit(solution)/shard_map/all_to_all | solution.py:209
  131.7 4.5 %collective-permute-start.18 = (bf16[512,128]{1,0:T(8,128)(2,1)S(1)}, bf16[512,128]{1,0:T(8,128)(2,1)S(1)}, u32[]{:S(2)}, u32[]{:S(2)}) collective-permute-start(bf16[512,128]{1,0:T(8,128)(2,1)S(1)} %get-tuple-element.61), channel_id=1, source_target_pairs={{0,64},{64,0},{1,65},{65,1},{2,66},{66,2},{3,67},{67,3},{4,68},{68... | collective-permute-start | bytes 393224 | tf_op jit(solution)/shard_map/ppermute | solution.py:205
  136.8 13.7 %all-to-all-start.2 = ((bf16[32,16,128]{2,1,0:T(8,128)(2,1)}), bf16[32,16,128]{2,1,0:T(8,128)(2,1)S(1)}, u32[]{:S(2)}, u32[]{:S(2)}) async-start(bf16[32,16,128]{2,1,0:T(8,128)(2,1)} %bitcast.10), calls=%async_computation.2 | async-start | bytes 262144 | tf_op jit(solution)/shard_map/all_to_all | solution.py:209
  150.5 3.7 %collective-permute-start.21 = (f32[16,128]{1,0:T(8,128)S(1)}, f32[16,128]{1,0:T(8,128)S(1)}, u32[]{:S(2)}, u32[]{:S(2)}) collective-permute-start(f32[16,128]{1,0:T(8,128)S(1)} %convert_reduce_fusion), channel_id=1, source_target_pairs={{0,129},{1,0},{128,1},{129,128},{2,131},{3,2},{130,3},{131,130},{4... | collective-permute-start | bytes 24584 | tf_op jit(solution)/shard_map/ppermute | solution.py:201
  153.0 3.7 %collective-permute-start.20 = (f32[16,128]{1,0:T(8,128)S(1)}, f32[16,128]{1,0:T(8,128)S(1)}, u32[]{:S(2)}, u32[]{:S(2)}) collective-permute-start(f32[16,128]{1,0:T(8,128)S(1)} %convert_reduce_fusion), channel_id=1, source_target_pairs={{0,1},{1,128},{128,129},{129,0},{2,3},{3,130},{130,131},{131,2},{4... | collective-permute-start | bytes 24584 | tf_op jit(solution)/shard_map/ppermute | solution.py:201
  153.0 4.0 %collective-permute-start.19 = (f32[16,128]{1,0:T(8,128)S(1)}, f32[16,128]{1,0:T(8,128)S(1)}, u32[]{:S(2)}, u32[]{:S(2)}) collective-permute-start(f32[16,128]{1,0:T(8,128)S(1)} %convert_reduce_fusion), channel_id=1, source_target_pairs={{0,128},{1,129},{128,0},{129,1},{2,130},{3,131},{130,2},{131,3},{4... | collective-permute-start | bytes 24584 | tf_op jit(solution)/shard_map/ppermute | solution.py:201
  170.1 5.1 %collective-permute-start.22 = (bf16[512,128]{1,0:T(8,128)(2,1)S(1)}, bf16[512,128]{1,0:T(8,128)(2,1)S(1)}, u32[]{:S(2)}, u32[]{:S(2)}) collective-permute-start(bf16[512,128]{1,0:T(8,128)(2,1)S(1)} %bitcast.28), channel_id=1, source_target_pairs={{0,64},{64,0},{1,65},{65,1},{2,66},{66,2},{3,67},{67,3},{4,68},{68... | collective-permute-start | bytes 393224 | tf_op jit(solution)/shard_map/ppermute | solution.py:205
  (13 other events, 125.1 us)

commit v2 on v1

--- a/solution.py
+++ b/solution.py
@@ -14,6 +14,7 @@
 f32 = jnp.float32
 Y = ("yh", "yl")
 ZX = ("z", "x")
+PLANE = ("yh", "core", "x", "yl")
 CORE_SWAP = [(0, 1), (1, 0)]
 MIB = 1 << 20
 
@@ -61,7 +62,6 @@
     return jax.ShapeDtypeStruct(dims, dtype)
 
 
-SMEM = pl.BlockSpec(memory_space=pltpu.SMEM)
 VMEM = pl.BlockSpec(memory_space=pltpu.VMEM)
 ANY = pl.BlockSpec(memory_space=pl.ANY)
 
@@ -78,7 +78,7 @@
 
 
 def prep_kernel(
-    place_ref, params_hbm, tokens_hbm, out_grad_hbm, message_ref, dispatch_ref, combine_ref,
+    params_hbm, tokens_hbm, out_grad_hbm, message_ref, dispatch_ref, combine_ref,
     params_ref, tokens_ref, out_grad_ref, sems,
 ):
     frames = tokens_ref.shape[0]
@@ -87,7 +87,7 @@
     copies += [load(tokens_hbm.at[f], tokens_ref.at[f], sems, f) for f in range(frames)]
     copies += [load(out_grad_hbm.at[f], out_grad_ref.at[f], sems, frames + f) for f in range(frames)]
     order = one_hot(
-        message_rows((rows, rows), 0, place_ref[0], frames, 2)
+        message_rows((rows, rows), 0, lax.axis_index("yl"), frames, 2)
         == lax.broadcasted_iota(jnp.int32, (rows, rows), 1)
     )
     copies[0].wait()
@@ -139,34 +139,31 @@
     message_ref[...] = dot(order, value).astype(bf16)
 
 
-def hidden_kernel(*refs):
-    pieces, w_in_ref, rows_ref, active_ref, slope_ref = refs[:8], *refs[8:]
-    rows = jnp.concatenate([piece[0] for piece in pieces], axis=0)
+def expert_kernel(count, *refs):
+    pieces, w_in_ref, w_out_ref = refs[:count], refs[count], refs[count + 1]
+    rows_ref, grads_ref, active_ref, pre_ref, partial_ref = refs[-5:]
+    rows = jnp.concatenate([piece[0, 0] for piece in pieces], axis=0)
+    grads = jnp.concatenate([piece[1, 0] for piece in pieces], axis=0)
     rows_ref[0] = rows
+    grads_ref[0] = grads
     hidden = dot(rows, w_in_ref[0])
+    act_grad = dot(grads, w_out_ref[0], ((1,), (1,)))
     cdf = 0.5 * (1.0 + lax.erf(hidden * inv_root_two))
     dens = jnp.exp(-0.5 * hidden * hidden) * inv_root_tau
     active_ref[0] = (hidden * cdf).astype(bf16)
-    slope_ref[0] = (cdf + hidden * dens).astype(slope_ref.dtype)
-
-
-def expert_kernel(*refs):
-    pieces, slope_ref, w_in_ref, w_out_ref = refs[:4], refs[4], refs[5], refs[6]
-    rows_ref, pre_ref, partial_ref = refs[-3:]
-    rows = jnp.concatenate([piece[0] for piece in pieces], axis=0)
-    rows_ref[0] = rows
-    act_grad = dot(rows, w_out_ref[0], ((1,), (1,)))
-    pre = (act_grad * slope_ref[0].astype(f32)).astype(bf16)
+    pre = (act_grad * (cdf + hidden * dens)).astype(bf16)
     pre_ref[0] = pre
     partial = dot(pre, w_in_ref[0], ((1,), (1,)))
     partial_ref[...] = partial.astype(partial_ref.dtype).reshape(partial_ref.shape)
 
 
-def tail_kernel(place_ref, message_ref, tokens_ref, dispatch_ref, part_ref, slots_ref, low_ref, mine_ref, theirs_ref, sum_ref):
+def tail_kernel(
+    message_ref, tokens_ref, dispatch_ref, part_ref, slots_ref, low_ref, total_ref
+):
     rows, depth = message_ref.shape
     frames, experts = slots_ref.shape[:2]
     order = one_hot(
-        message_rows((rows, rows), 1, place_ref[0], frames, 1)
+        message_rows((rows, rows), 1, lax.axis_index("yl"), frames, 1)
         == lax.broadcasted_iota(jnp.int32, (rows, rows), 0)
     )
     slots = dot(order, message_ref[...]).astype(bf16)
@@ -182,11 +179,7 @@
         low_ref[f] = low
         term = dot(low, tokens, ((0,), (0,)))
         total = term if total is None else total + term
-    sum_ref[...] = total.T
-    half = depth // 2
-    core = place_ref[1]
-    mine_ref[...] = sum_ref[pl.ds(pl.multiple_of(core * half, half), half), :]
-    theirs_ref[...] = sum_ref[pl.ds(pl.multiple_of((1 - core) * half, half), half), :].astype(bf16)
+    total_ref[...] = total.T.astype(bf16)
 
 
 def tokens_kernel(dispatch_ref, low_ref, slots_ref, params_ref, out_ref):
@@ -205,24 +198,20 @@
     return lax.ppermute(value, "core", CORE_SWAP)
 
 
-def exchange(value):
-    return lax.all_to_all(value, ZX, split_axis=0, concat_axis=0, tiled=True)
-
-
-def sum_all(mine, theirs, groups, beside):
-    half, cols = mine.shape
-    core = lax.axis_index("core")
-    mine = (mine + to_core(theirs).astype(f32)).astype(bf16)
-    pieces = exchange(mine.reshape(groups, half // groups, cols))
-    pieces, beside = lax.optimization_barrier((pieces, beside))
-    part = jnp.sum(pieces.astype(f32), axis=0)
-    across, back, ahead = to_y(part, 2), to_y(part, 1), to_y(part, -1)
-    total = ((part + across) + (back + ahead)).astype(bf16)
-    mine = exchange(jnp.broadcast_to(total[None], (groups,) + total.shape)).reshape(half, cols)
-    theirs = to_core(mine)
-    low = jnp.where(core == 0, mine, theirs)
-    high = jnp.where(core == 0, theirs, mine)
-    return jnp.concatenate([low, high], axis=0).astype(f32), beside
+def exchange(value, axes=ZX):
+    return lax.all_to_all(value, axes, split_axis=0, concat_axis=0, tiled=True)
+
+
+def sum_all(value, beside):
+    rows, cols = value.shape
+    peers, height = lax.axis_size(PLANE), lax.axis_size("z")
+    value = exchange(value.reshape(peers, rows // peers, cols), PLANE)
+    value, beside = lax.optimization_barrier((value, beside))
+    value = jnp.sum(value.astype(f32), axis=0).astype(bf16)
+    value = exchange(jnp.broadcast_to(value[None], (height,) + value.shape), "z")
+    value = jnp.sum(value.astype(f32), axis=0).astype(bf16)
+    value = exchange(jnp.broadcast_to(value[None], (peers,) + value.shape), PLANE)
+    return value.reshape(rows, cols).astype(f32), beside
 
 
 def shards(tokens, slot_params, w_in, w_out, slot_outputs, out_grad):
@@ -232,7 +221,6 @@
     groups = experts // 4
     rows = frames * experts
     block = rows // 4
-    place = jnp.stack([lax.axis_index("yl"), lax.axis_index("core")]).astype(jnp.int32)
     frame_flops = 2 * frames * patch * experts * depth
     sort_flops = 2 * rows * rows * depth
 
@@ -243,8 +231,8 @@
             shape((frames, patch, experts), f32),
             shape((frames, patch, experts), f32),
         ),
-        place, slot_params, tokens, out_grad,
-        in_specs=[SMEM, ANY, ANY, ANY], vmem=56, flops=3 * frame_flops + 4 * sort_flops,
+        slot_params, tokens, out_grad,
+        in_specs=[ANY, ANY, ANY], vmem=56, flops=3 * frame_flops + 4 * sort_flops,
         scratch_shapes=[
             pltpu.VMEM((depth, experts), bf16),
             pltpu.VMEM((frames, patch, depth), bf16),
@@ -262,65 +250,48 @@
     )
     message, combine_part = lax.optimization_barrier((message, combine_part))
 
-    own_in, own_grad, other_in, other_grad = call(
-        functools.partial(sort_kernel, frames), (shape((2, block, depth), bf16),) * 4, message,
+    own, other = call(
+        functools.partial(sort_kernel, frames), (shape((2, 2, block, depth), bf16),) * 2, message,
         flops=4 * sort_flops,
     )
-    near_in = [own_in, to_y(other_in, 1), to_y(other_in, -1), to_y(own_in, 2)]
-    near_grad = [own_grad, to_y(other_grad, 1), to_y(other_grad, -1), to_y(own_grad, 2)]
-    far_in = [to_core(piece) for piece in near_in]
-    far_own = to_core(own_grad)
-
-    piece = pl.BlockSpec((1, block, depth), lambda e: (e, 0, 0))
+    near = [own, to_y(other, 1), to_y(other, -1), to_y(own, 2)]
+    far = [to_core(piece) for piece in near]
+
+    piece = pl.BlockSpec((2, 1, block, depth), lambda e: (0, e, 0, 0))
     w_in_spec = pl.BlockSpec((1, depth, hidden_size), lambda e: (e, 0, 0))
     w_out_spec = pl.BlockSpec((1, hidden_size, depth), lambda e: (e, 0, 0))
-    matmul_flops = 2 * 2 * 8 * block * depth * hidden_size
-    slot_rows, active, slope = call(
-        hidden_kernel,
-        (
-            shape((2, 8 * block, depth), bf16),
-            shape((2, 8 * block, hidden_size), bf16),
-            shape((2, 8 * block, hidden_size), bf16),
-        ),
-        *near_in, *far_in, w_in,
-        grid=(2,),
-        in_specs=[piece] * 8 + [w_in_spec],
-        out_specs=(
-            pl.BlockSpec((1, 8 * block, depth), lambda e: (e, 0, 0)),
-            pl.BlockSpec((1, 8 * block, hidden_size), lambda e: (e, 0, 0)),
-            pl.BlockSpec((1, 8 * block, hidden_size), lambda e: (e, 0, 0)),
-        ),
-        vmem=24, flops=matmul_flops,
-    )
-    slope, *arrived = lax.optimization_barrier((slope, *near_grad[1:]))
-    near_grad = [own_grad, *arrived]
-    far_grad = [far_own] + [to_core(piece) for piece in arrived]
+    matmul_flops = 2 * 2 * 4 * block * depth * hidden_size
 
     def expert_half(half, pieces, filled):
         rows_spec = pl.BlockSpec((1, 4 * block, depth), lambda e: (e, half, 0))
         hidden_spec = pl.BlockSpec((1, 4 * block, hidden_size), lambda e: (e, half, 0))
         return call(
-            expert_kernel,
+            functools.partial(expert_kernel, 4),
             (
                 shape((2, 8 * block, depth), bf16),
+                shape((2, 8 * block, depth), bf16),
+                shape((2, 8 * block, hidden_size), bf16),
                 shape((2, 8 * block, hidden_size), bf16),
                 shape((4, 2, block, depth), bf16 if half else f32),
             ),
-            *pieces, slope, w_in, w_out, *filled,
+            *pieces, w_in, w_out, *filled,
             grid=(2,),
-            in_specs=[piece] * 4 + [hidden_spec, w_in_spec, w_out_spec] + [ANY] * len(filled),
+            in_specs=[piece] * 4 + [w_in_spec, w_out_spec] + [ANY] * len(filled),
             out_specs=(
                 rows_spec,
+                rows_spec,
+                hidden_spec,
                 hidden_spec,
                 pl.BlockSpec((4, 1, block, depth), lambda e: (0, e, 0, 0)),
             ),
-            vmem=24, flops=matmul_flops,
-            input_output_aliases={7 + i: i for i in range(len(filled))},
+            vmem=24, flops=3 * matmul_flops,
+            input_output_aliases={6 + i: i for i in range(len(filled))},
         )
 
-    *filled, far = expert_half(1, far_grad, ())
+    *filled, near = expert_half(0, near, ())
+    near, far[1] = lax.optimization_barrier((near, far[1]))
+    slot_rows, grad_rows, active, pre_grad, far = expert_half(1, far, filled)
     far = to_core(far)
-    grad_rows, pre_grad, near = expert_half(0, near_grad, filled)
 
     def summed(i):
         return (near[i] + far[i].astype(f32)).astype(bf16)
@@ -341,24 +312,20 @@
     message = exchange(message.reshape(groups, rows // groups, depth)).reshape(rows, depth)
     message, w_out_grad = lax.optimization_barrier((message, w_out_grad))
 
-    slots_in_grad, logits_low, mine, theirs = call(
+    slots_in_grad, logits_low, total = call(
         tail_kernel,
         (
             shape((frames, experts, depth), bf16),
             shape((frames, patch, experts), bf16),
-            shape((depth // 2, experts), f32),
-            shape((depth // 2, experts), bf16),
+            shape((depth, experts), bf16),
         ),
-        place, message, tokens, dispatch, combine_part,
-        in_specs=[SMEM, VMEM, VMEM, VMEM, VMEM],
-        scratch_shapes=[pltpu.VMEM((depth, experts), f32)],
-        flops=2 * frame_flops + sort_flops,
+        message, tokens, dispatch, combine_part, flops=2 * frame_flops + sort_flops,
     )
     tokens_grad = call(
         tokens_kernel, shape((frames, patch, depth), bf16),
         dispatch, logits_low, slots_in_grad, slot_params, flops=2 * frame_flops,
     )
-    params_grad, tokens_grad = sum_all(mine, theirs, groups, tokens_grad)
+    params_grad, tokens_grad = sum_all(total, tokens_grad)
     return (tokens_grad, params_grad, w_in_grad, w_out_grad)
 
 

time: 177 us -> 170 us (0.960)
  blocking collectives: 13.1 us -> 23.6 us
  starting transfers between devices: 59.8 us -> 50.8 us
  waiting for transfers between devices: 63.9 us -> 58.4 us
    all_to_all x1 -> x2, blocking collectives: 13.1 us -> 23.6 us  [exchange(): return lax.all_to_all(value, axes, split_axis=0, concat_axis=0, tiled=True)]
    ppermute x11 -> x5, starting transfers between devices: 24.3 us -> 16.2 us  [to_core(): return lax.ppermute(value, 'core', CORE_SWAP)]
    ppermute x12 -> x6, starting transfers between devices: 12.9 us -> 7.61 us  [to_y(): return lax.ppermute(value, Y, [(i, (i + step) % 4) for i in range(4)])]
    all_to_all x3, starting transfers between devices: 22.5 us -> 27 us  [exchange(): return lax.all_to_all(value, axes, split_axis=0, concat_axis=0, tiled=True)]
    ppermute x12 -> x6, waiting for transfers between devices: 20.2 us -> 15.9 us  [to_y(): return lax.ppermute(value, Y, [(i, (i + step) % 4) for i in range(4)])]
    pallas_call x8 -> x7, Pallas kernels: 19.5 us -> 18.4 us  [call(): pl.pallas_call(kernel, out_shape=out_shape, grid=grid, in_specs=in_specs,...]
    unnamed x22 -> x20, local copies, waits for them, and re-layouts: 6.13 us -> 5.84 us
  transfers between devices with their start and end apart: 26 -> 14, of which waited for: 13 -> 7; matrix products, arithmetic and copies ran while one was open for 6% -> 6% of each run, Pallas kernels for 4% -> 3%
where the time goes in v2:
time: 170 us
  waiting for transfers between devices  58.4 us (34%)
  starting transfers between devices  50.8 us (30%)
  blocking collectives  23.6 us (14%)
  Pallas kernels  18.4 us (11%)
  matrix products  10.3 us (6%)
  local copies, waits for them, and re-layouts  5.89 us (3%)
    all_to_all x3, waiting for transfers between devices, exchange(): return lax.all_to_all(value, axes, split_axis=0, concat_axis=0, tiled=True)  39.8 us
    all_to_all x3, starting transfers between devices, exchange(): return lax.all_to_all(value, axes, split_axis=0, concat_axis=0, tiled=True)  27 us
    all_to_all x2, blocking collectives, exchange(): return lax.all_to_all(value, axes, split_axis=0, concat_axis=0, tiled=True)  23.6 us
    pallas_call x7, Pallas kernels, call(): pl.pallas_call(kernel, out_shape=out_shape, grid=grid, in_specs=in_specs,...  18.4 us
    ppermute x5, starting transfers between devices, to_core(): return lax.ppermute(value, 'core', CORE_SWAP)  16.2 us
    ppermute x6, waiting for transfers between devices, to_y(): return lax.ppermute(value, Y, [(i, (i + step) % 4) for i in range(4)])  15.9 us
    ppermute x6, starting transfers between devices, to_y(): return lax.ppermute(value, Y, [(i, (i + step) % 4) for i in range(4)])  7.61 us
    unnamed x20, local copies, waits for them, and re-layouts  5.84 us
  transfers between devices with their start and end apart: 14, of which 7 were waited for; matrix products, arithmetic and copies ran while one was open for 6% of the time, Pallas kernels for 3%

profile of v2, /device:TPU:1, one launch (start us, length us, event | category | flops | bytes accessed | tf_op | source)
XLA Modules:
  0.0 169.5 jit_solution(14122974747960774223)
XLA Ops:
  0.6 4.5 %shard_map.93 = (bf16[512,1024]{1,0:T(8,128)(2,1)}, f32[2,256,128]{2,1,0:T(8,128)}, f32[2,256,128]{2,1,0:T(8,128)}) custom-call(bf16[1024,128]{1,0:T(8,128)(2,1)} %params_ref.1, bf16[2,256,1024]{2,1,0:T(8,128)(2,1)} %tokens_ref.1, bf16[2,256,1024]{2,1,0:T(8,128)(2,1)} %out_grad_hbm.1), custom_call_target="tpu_custom_call" | custom-call | flops 939524096 | bytes 3932160 | tf_op jit(solution)/shard_map/pallas_call | solution.py:49
  5.1 12.0 %all-to-all-start = ((bf16[32,16,1024]{2,1,0:T(8,128)(2,1)}), bf16[32,16,1024]{2,1,0:T(8,128)(2,1)}, u32[]{:S(2)}, u32[]{:S(2)}) async-start(bf16[32,16,1024]{2,1,0:T(8,128)(2,1)} %bitcast.25), calls=%async_computation | async-start | bytes 2097152 | tf_op jit(solution)/shard_map/all_to_all | solution.py:202
  17.2 2.6 %fusion.2.part_ref = f32[2,256,128]{2,1,0:T(8,128)S(1)} fusion(f32[2,256,128]{2,1,0:T(8,128)} %get-tuple-element.33, bf16[2,256,1024]{2,1,0:T(8,128)(2,1)} %out_grad_hbm.1, bf16[2,128,1024]{2,1,0:T(8,128)(2,1)S(1)} %copy-done), kind=kOutput, calls=%fused_computation.4 | convolution fusion | flops 268632704 | bytes 2097152 | tf_op jit(solution)/shard_map/sub | solution.py:249
  19.7 23.6 %all-to-all-done = bf16[32,16,1024]{2,1,0:T(8,128)(2,1)} async-done(((bf16[32,16,1024]{2,1,0:T(8,128)(2,1)}), bf16[32,16,1024]{2,1,0:T(8,128)(2,1)}, u32[]{:S(2)}, u32[]{:S(2)}) %all-to-all-start) | async-done | bytes 1048608 | tf_op jit(solution)/shard_map/all_to_all | solution.py:202
  43.3 2.1 %shard_map.94 = (bf16[2,2,64,1024]{3,2,1,0:T(8,128)(2,1)S(1)}, bf16[2,2,64,1024]{3,2,1,0:T(8,128)(2,1)S(1)}) custom-call(bf16[512,1024]{1,0:T(8,128)(2,1)} %bitcast.1.message_ref), custom_call_target="tpu_custom_call" | custom-call | flops 536870912 | bytes 2097152 | tf_op jit(solution)/shard_map/pallas_call | solution.py:49
  49.9 7.5 %collective-permute-done.refs_1_ = bf16[2,2,64,1024]{3,2,1,0:T(8,128)(2,1)S(1)} collective-permute-done((bf16[2,2,64,1024]{3,2,1,0:T(8,128)(2,1)S(1)}, bf16[2,2,64,1024]{3,2,1,0:T(8,128)(2,1)S(1)}, u32[]{:S(2)}, u32[]{:S(2)}) %collective-permute-start) | collective-permute-done | bytes 524320 | tf_op jit(solution)/shard_map/ppermute | solution.py:194
  57.4 5.9 %collective-permute-start.3 = (bf16[2,2,64,1024]{3,2,1,0:T(8,128)(2,1)S(1)}, bf16[2,2,64,1024]{3,2,1,0:T(8,128)(2,1)S(1)}, u32[]{:S(2)}, u32[]{:S(2)}) collective-permute-start(bf16[2,2,64,1024]{3,2,1,0:T(8,128)(2,1)S(1)} %collective-permute-done.refs_1_), channel_id=1, source_target_pairs={{0,64},{64,0},{1,65},{65,1},{2,66},{66,2},{3,67},{67,3},{4,68},{68... | collective-permute-start | bytes 1572872 | tf_op jit(solution)/shard_map/ppermute | solution.py:198
  63.3 8.4 %collective-permute-start.5 = (bf16[2,2,64,1024]{3,2,1,0:T(8,128)(2,1)S(1)}, bf16[2,2,64,1024]{3,2,1,0:T(8,128)(2,1)S(1)}, u32[]{:S(2)}, u32[]{:S(2)}) collective-permute-start(bf16[2,2,64,1024]{3,2,1,0:T(8,128)(2,1)S(1)} %collective-permute-done.1.refs_2_), channel_id=1, source_target_pairs={{0,64},{64,0},{1,65},{65,1},{2,66},{66,2},{3,67},{67,3},{4,68},{68... | collective-permute-start | bytes 1572872 | tf_op jit(solution)/shard_map/ppermute | solution.py:198
  71.7 1.8 %collective-permute-start.6 = (bf16[2,2,64,1024]{3,2,1,0:T(8,128)(2,1)S(1)}, bf16[2,2,64,1024]{3,2,1,0:T(8,128)(2,1)S(1)}, u32[]{:S(2)}, u32[]{:S(2)}) collective-permute-start(bf16[2,2,64,1024]{3,2,1,0:T(8,128)(2,1)S(1)} %collective-permute-done.2.refs_3_), channel_id=1, source_target_pairs={{0,64},{64,0},{1,65},{65,1},{2,66},{66,2},{3,67},{67,3},{4,68},{68... | collective-permute-start | bytes 1572872 | tf_op jit(solution)/shard_map/ppermute | solution.py:198
  75.3 3.8 %shard_map.95 = (bf16[2,512,1024]{2,1,0:T(8,128)(2,1)S(1)}, bf16[2,512,1024]{2,1,0:T(8,128)(2,1)S(1)}, bf16[2,512,640]{2,1,0:T(8,128)(2,1)S(1)}, bf16[2,512,640]{2,1,0:T(8,128)(2,1)S(1)}, f32[4,2,64,1024]{3,2,1,0:T(8,128)S(1)}) custom-call(bf16[2,2,64,1024]{3,2,1,0:T(8,128)(2,1)S(1)} %get-tuple-element.35.refs_0_, ...), custom_call_target="tpu_custom_call" | custom-call | flops 2013265920 | bytes 16252928 | tf_op jit(solution)/shard_map/pallas_call | solution.py:49
  79.1 3.7 %shard_map.96 = (bf16[2,512,1024]{2,1,0:T(8,128)(2,1)S(1)}, bf16[2,512,1024]{2,1,0:T(8,128)(2,1)S(1)}, bf16[2,512,640]{2,1,0:T(8,128)(2,1)S(1)}, bf16[2,512,640]...) custom-call(bf16[2,2,64,1024]{3,2,1,0:T(8,128)(2,1)S(1)} %collective, ...), custom_call_target="tpu_custom_call", output_to_operand_aliasing={{0}: (6, {}), {1}: (7, {}), {2}: (8, {}), {3}: (9, {})} | custom-call | flops 2013265920 | bytes 22020096 | tf_op jit(solution)/shard_map/pallas_call | solution.py:49
  82.9 2.6 %collective-permute-done.7 = bf16[4,2,64,1024]{3,2,1,0:T(8,128)(2,1)S(1)} collective-permute-done((bf16[4,2,64,1024]{3,2,1,0:T(8,128)(2,1)S(1)}, bf16[4,2,64,1024]{3,2,1,0:T(8,128)(2,1)S(1)}, u32[]{:S(2)}, u32[]{:S(2)}) %collective-permute-start.7) | collective-permute-done | bytes 1048608 | tf_op jit(solution)/shard_map/ppermute | solution.py:198
  87.1 1.8 %collective-permute-start.9 = (bf16[2,64,1024]{2,1,0:T(8,128)(2,1)S(1)}, bf16[2,64,1024]{2,1,0:T(8,128)(2,1)S(1)}, u32[]{:S(2)}, u32[]{:S(2)}) collective-permute-start(bf16[2,64,1024]{2,1,0:T(8,128)(2,1)S(1)} %get-tuple-element.61), channel_id=1, source_target_pairs={{0,129},{1,0},{128,1},{129,128},{2,131},{3,2},{130,3},{131,130},{4... | collective-permute-start | bytes 786440 | tf_op jit(solution)/shard_map/ppermute | solution.py:194
  89.1 3.3 %convolution_convert_fusion.1 = bf16[2,1024,640]{2,1,0:T(8,128)(2,1)} fusion(bf16[2,512,1024]{2,1,0:T(8,128)(2,1)S(1)} %get-tuple-element.45, bf16[2,512,640]{2,1,0:T(8,128)(2,1)S(1)} %get-tuple-element.46), kind=kOutput, calls=%fused_computation.2 | convolution fusion | flops 1343488000 | bytes 6029312 | tf_op jit(solution)/shard_map/erd,erh->edh/dot_general | solution.py:304
  92.5 2.8 %collective-permute-done.10.ahead_ref = bf16[2,64,1024]{2,1,0:T(8,128)(2,1)S(1)} collective-permute-done((bf16[2,64,1024]{2,1,0:T(8,128)(2,1)S(1)}, bf16[2,64,1024]{2,1,0:T(8,128)(2,1)S(1)}, u32[]{:S(2)}, u32[]{:S(2)}) %collective-permute-start.10) | collective-permute-done | bytes 262176 | tf_op jit(solution)/shard_map/ppermute | solution.py:194
  95.2 5.6 %collective-permute-done.8.across_ref = bf16[2,64,1024]{2,1,0:T(8,128)(2,1)S(1)} collective-permute-done((bf16[2,64,1024]{2,1,0:T(8,128)(2,1)S(1)}, bf16[2,64,1024]{2,1,0:T(8,128)(2,1)S(1)}, u32[]{:S(2)}, u32[]{:S(2)}) %collective-permute-start.8) | collective-permute-done | bytes 262176 | tf_op jit(solution)/shard_map/ppermute | solution.py:194
  101.9 6.4 %all-to-all-start.1 = ((bf16[32,8,1024]{2,1,0:T(8,128)(2,1)}), bf16[32,8,1024]{2,1,0:T(8,128)(2,1)S(1)}, u32[]{:S(2)}, u32[]{:S(2)}) async-start(bf16[32,8,1024]{2,1,0:T(8,128)(2,1)} %bitcast.6), calls=%async_computation.1 | async-start | bytes 1048576 | tf_op jit(solution)/shard_map/all_to_all | solution.py:202
  108.3 4.4 %convolution_convert_fusion = bf16[2,640,1024]{2,1,0:T(8,128)(2,1)} fusion(bf16[2,512,640]{2,1,0:T(8,128)(2,1)} %copy-done.5, bf16[2,512,1024]{2,1,0:T(8,128)(2,1)S(1)} %copy-done.4), kind=kOutput, calls=%fused_computation.1 | convolution fusion | flops 1343488000 | bytes 6029312 | tf_op jit(solution)/shard_map/erh,erd->ehd/dot_general | solution.py:301
  112.7 11.0 %all-to-all-done.1 = bf16[32,8,1024]{2,1,0:T(8,128)(2,1)S(1)} async-done(((bf16[32,8,1024]{2,1,0:T(8,128)(2,1)}), bf16[32,8,1024]{2,1,0:T(8,128)(2,1)S(1)}, u32[]{:S(2)}, u32[]{:S(2)}) %all-to-all-start.1) | async-done | bytes 524320 | tf_op jit(solution)/shard_map/all_to_all | solution.py:202
  125.8 1.8 %shard_map.98 = (bf16[2,128,1024]{2,1,0:T(8,128)(2,1)S(1)}, bf16[2,256,128]{2,1,0:T(8,128)(2,1)S(1)}, bf16[1024,128]{1,0:T(8,128)(2,1)}) custom-call(bf16[256,1024]{1,0:T(8,128)(2,1)S(1)} %bitcast.24, bf16[2,256,1024]{2,1,0:T(8,128)(2,1)S(1)} %copy-done.6, f32[2,256,128]{2,1,0:T(8,128)S(1)} %copy-done.7, f32[2,256,128]{2,1,0:T(8,128)S(1)} %fusion.2.part_ref), custom_call_target="tpu_custom_call" | custom-call | flops 402653184 | bytes 3014656 | tf_op jit(solution)/shard_map/pallas_call | solution.py:49
  127.6 8.7 %all-to-all-start.2 = ((bf16[32,32,128]{2,1,0:T(8,128)(2,1)}), bf16[32,32,128]{2,1,0:T(8,128)(2,1)S(1)}, u32[]{:S(2)}, u32[]{:S(2)}) async-start(bf16[32,32,128]{2,1,0:T(8,128)(2,1)} %bitcast.8), calls=%async_computation.2 | async-start | bytes 524288 | tf_op jit(solution)/shard_map/all_to_all | solution.py:202
  139.6 5.3 %all-to-all-done.2 = bf16[32,32,128]{2,1,0:T(8,128)(2,1)S(1)} async-done(((bf16[32,32,128]{2,1,0:T(8,128)(2,1)}), bf16[32,32,128]{2,1,0:T(8,128)(2,1)S(1)}, u32[]{:S(2)}, u32[]{:S(2)}) %all-to-all-start.2) | async-done | bytes 262176 | tf_op jit(solution)/shard_map/all_to_all | solution.py:202
  145.0 9.6 %all_to_all.25 = bf16[8,32,128]{2,1,0:T(8,128)(2,1)S(1)} all-to-all(bf16[8,32,128]{2,1,0:T(8,128)(2,1)S(1)} %broadcast_in_dim.4), channel_id=1, replica_groups=mesh['yh'=2,'core'=2,'z'=8,'x'=4,'yl'=2] {'z'}, dimensions={0} | all-to-all | bytes 131072 | tf_op jit(solution)/shard_map/all_to_all | solution.py:202
  154.6 14.0 %all_to_all.26 = bf16[32,32,128]{2,1,0:T(8,128)(2,1)S(1)} all-to-all(bf16[32,32,128]{2,1,0:T(8,128)(2,1)S(1)} %broadcast_in_dim.5), channel_id=1, replica_groups=mesh['yh'=2,'core'=2,'z'=8,'x'=4,'yl'=2] {'yh','core','x','yl'}, dimensions={0} | all-to-all | bytes 524288 | tf_op jit(solution)/shard_map/all_to_all | solution.py:202
  (42 shorter events, 15.7 us)
Async XLA Ops:
  0.6 16.5 %copy-start = (bf16[2,128,1024]{2,1,0:T(8,128)(2,1)S(1)}, bf16[2,128,1024]{2,1,0:T(8,128)(2,1)}, u32[]{:S(2)}) copy-start(bf16[2,128,1024]{2,1,0:T(8,128)(2,1)} %param.10) | copy-start | bytes 1572868
  5.1 38.2 %all-to-all-start = ((bf16[32,16,1024]{2,1,0:T(8,128)(2,1)}), bf16[32,16,1024]{2,1,0:T(8,128)(2,1)}, u32[]{:S(2)}, u32[]{:S(2)}) async-start(bf16[32,16,1024]{2,1,0:T(8,128)(2,1)} %bitcast.25), calls=%async_computation | async-start | bytes 2097152 | tf_op jit(solution)/shard_map/all_to_all | solution.py:202
  17.2 56.4 %copy-start.1 = (bf16[2,1024,640]{2,1,0:T(8,128)(2,1)S(1)}, bf16[2,1024,640]{2,1,0:T(8,128)(2,1)}, u32[]{:S(2)}) copy-start(bf16[2,1024,640]{2,1,0:T(8,128)(2,1)} %refs_4_.3) | copy-start | bytes 7864324
  45.4 12.0 %collective-permute-start = (bf16[2,2,64,1024]{3,2,1,0:T(8,128)(2,1)S(1)}, bf16[2,2,64,1024]{3,2,1,0:T(8,128)(2,1)S(1)}, u32[]{:S(2)}, u32[]{:S(2)}) collective-permute-start(bf16[2,2,64,1024]{3,2,1,0:T(8,128)(2,1)S(1)} %get-tuple-element.36), channel_id=1, source_target_pairs={{0,1},{1,128},{128,129},{129,0},{2,3},{3,130},{130,131},{131,2},{4... | collective-permute-start | bytes 1572872 | tf_op jit(solution)/shard_map/ppermute | solution.py:194
  46.8 16.5 %collective-permute-start.1 = (bf16[2,2,64,1024]{3,2,1,0:T(8,128)(2,1)S(1)}, bf16[2,2,64,1024]{3,2,1,0:T(8,128)(2,1)S(1)}, u32[]{:S(2)}, u32[]{:S(2)}) collective-permute-start(bf16[2,2,64,1024]{3,2,1,0:T(8,128)(2,1)S(1)} %get-tuple-element.36), channel_id=1, source_target_pairs={{0,129},{1,0},{128,1},{129,128},{2,131},{3,2},{130,3},{131,130},{4... | collective-permute-start | bytes 1572872 | tf_op jit(solution)/shard_map/ppermute | solution.py:194
  48.3 23.4 %collective-permute-start.2 = (bf16[2,2,64,1024]{3,2,1,0:T(8,128)(2,1)S(1)}, bf16[2,2,64,1024]{3,2,1,0:T(8,128)(2,1)S(1)}, u32[]{:S(2)}, u32[]{:S(2)}) collective-permute-start(bf16[2,2,64,1024]{3,2,1,0:T(8,128)(2,1)S(1)} %get-tuple-element.35.refs_0_), channel_id=1, source_target_pairs={{0,128},{1,129},{128,0},{129,1},{2,130},{3,131},{130,2},{131,3},{4... | collective-permute-start | bytes 1572872 | tf_op jit(solution)/shard_map/ppermute | solution.py:194
  57.4 21.6 %collective-permute-start.3 = (bf16[2,2,64,1024]{3,2,1,0:T(8,128)(2,1)S(1)}, bf16[2,2,64,1024]{3,2,1,0:T(8,128)(2,1)S(1)}, u32[]{:S(2)}, u32[]{:S(2)}) collective-permute-start(bf16[2,2,64,1024]{3,2,1,0:T(8,128)(2,1)S(1)} %collective-permute-done.refs_1_), channel_id=1, source_target_pairs={{0,64},{64,0},{1,65},{65,1},{2,66},{66,2},{3,67},{67,3},{4,68},{68... | collective-permute-start | bytes 1572872 | tf_op jit(solution)/shard_map/ppermute | solution.py:198
  63.3 15.8 %collective-permute-start.4 = (bf16[2,2,64,1024]{3,2,1,0:T(8,128)(2,1)S(1)}, bf16[2,2,64,1024]{3,2,1,0:T(8,128)(2,1)S(1)}, u32[]{:S(2)}, u32[]{:S(2)}) collective-permute-start(bf16[2,2,64,1024]{3,2,1,0:T(8,128)(2,1)S(1)} %get-tuple-element.35.refs_0_), channel_id=1, source_target_pairs={{0,64},{64,0},{1,65},{65,1},{2,66},{66,2},{3,67},{67,3},{4,68},{68... | collective-permute-start | bytes 1572872 | tf_op jit(solution)/shard_map/ppermute | solution.py:198
  63.3 15.8 %collective-permute-start.5 = (bf16[2,2,64,1024]{3,2,1,0:T(8,128)(2,1)S(1)}, bf16[2,2,64,1024]{3,2,1,0:T(8,128)(2,1)S(1)}, u32[]{:S(2)}, u32[]{:S(2)}) collective-permute-start(bf16[2,2,64,1024]{3,2,1,0:T(8,128)(2,1)S(1)} %collective-permute-done.1.refs_2_), channel_id=1, source_target_pairs={{0,64},{64,0},{1,65},{65,1},{2,66},{66,2},{3,67},{67,3},{4,68},{68... | collective-permute-start | bytes 1572872 | tf_op jit(solution)/shard_map/ppermute | solution.py:198
  71.7 7.3 %collective-permute-start.6 = (bf16[2,2,64,1024]{3,2,1,0:T(8,128)(2,1)S(1)}, bf16[2,2,64,1024]{3,2,1,0:T(8,128)(2,1)S(1)}, u32[]{:S(2)}, u32[]{:S(2)}) collective-permute-start(bf16[2,2,64,1024]{3,2,1,0:T(8,128)(2,1)S(1)} %collective-permute-done.2.refs_3_), channel_id=1, source_target_pairs={{0,64},{64,0},{1,65},{65,1},{2,66},{66,2},{3,67},{67,3},{4,68},{68... | collective-permute-start | bytes 1572872 | tf_op jit(solution)/shard_map/ppermute | solution.py:198
  73.5 1.7 %copy-start.2 = (bf16[2,640,1024]{2,1,0:T(8,128)(2,1)S(1)}, bf16[2,640,1024]{2,1,0:T(8,128)(2,1)}, u32[]{:S(2)}) copy-start(bf16[2,640,1024]{2,1,0:T(8,128)(2,1)} %refs_5_.3) | copy-start | bytes 7864324
  82.8 3.1 %copy-start.3 = (bf16[2,512,1024]{2,1,0:T(8,128)(2,1)}, bf16[2,512,1024]{2,1,0:T(8,128)(2,1)S(1)}, u32[]{:S(2)}) copy-start(bf16[2,512,1024]{2,1,0:T(8,128)(2,1)S(1)} %get-tuple-element.49) | copy-start | bytes 6291460
  82.8 3.1 %copy-start.5 = (bf16[2,512,640]{2,1,0:T(8,128)(2,1)}, bf16[2,512,640]{2,1,0:T(8,128)(2,1)S(1)}, u32[]{:S(2)}) copy-start(bf16[2,512,640]{2,1,0:T(8,128)(2,1)S(1)} %get-tuple-element.48) | copy-start | bytes 3932164
  82.8 2.7 %collective-permute-start.7 = (bf16[4,2,64,1024]{3,2,1,0:T(8,128)(2,1)S(1)}, bf16[4,2,64,1024]{3,2,1,0:T(8,128)(2,1)S(1)}, u32[]{:S(2)}, u32[]{:S(2)}) collective-permute-start(bf16[4,2,64,1024]{3,2,1,0:T(8,128)(2,1)S(1)} %get-tuple-element.44), channel_id=1, source_target_pairs={{0,64},{64,0},{1,65},{65,1},{2,66},{66,2},{3,67},{67,3},{4,68},{68... | collective-permute-start | bytes 3145736 | tf_op jit(solution)/shard_map/ppermute | solution.py:198
  86.0 9.3 %collective-permute-start.10 = (bf16[2,64,1024]{2,1,0:T(8,128)(2,1)S(1)}, bf16[2,64,1024]{2,1,0:T(8,128)(2,1)S(1)}, u32[]{:S(2)}, u32[]{:S(2)}) collective-permute-start(bf16[2,64,1024]{2,1,0:T(8,128)(2,1)S(1)} %get-tuple-element.60), channel_id=1, source_target_pairs={{0,1},{1,128},{128,129},{129,0},{2,3},{3,130},{130,131},{131,2},{4... | collective-permute-start | bytes 786440 | tf_op jit(solution)/shard_map/ppermute | solution.py:194
  87.1 8.1 %collective-permute-start.9 = (bf16[2,64,1024]{2,1,0:T(8,128)(2,1)S(1)}, bf16[2,64,1024]{2,1,0:T(8,128)(2,1)S(1)}, u32[]{:S(2)}, u32[]{:S(2)}) collective-permute-start(bf16[2,64,1024]{2,1,0:T(8,128)(2,1)S(1)} %get-tuple-element.61), channel_id=1, source_target_pairs={{0,129},{1,0},{128,1},{129,128},{2,131},{3,2},{130,3},{131,130},{4... | collective-permute-start | bytes 786440 | tf_op jit(solution)/shard_map/ppermute | solution.py:194
  88.9 11.9 %collective-permute-start.8 = (bf16[2,64,1024]{2,1,0:T(8,128)(2,1)S(1)}, bf16[2,64,1024]{2,1,0:T(8,128)(2,1)S(1)}, u32[]{:S(2)}, u32[]{:S(2)}) collective-permute-start(bf16[2,64,1024]{2,1,0:T(8,128)(2,1)S(1)} %get-tuple-element.62), channel_id=1, source_target_pairs={{0,128},{1,129},{128,0},{129,1},{2,130},{3,131},{130,2},{131,3},{4... | collective-permute-start | bytes 786440 | tf_op jit(solution)/shard_map/ppermute | solution.py:194
  92.5 15.9 %copy-start.4 = (bf16[2,512,1024]{2,1,0:T(8,128)(2,1)S(1)}, bf16[2,512,1024]{2,1,0:T(8,128)(2,1)}, u32[]{:S(2)}) copy-start(bf16[2,512,1024]{2,1,0:T(8,128)(2,1)} %copy-done.3) | copy-start | bytes 6291460
  101.9 21.7 %all-to-all-start.1 = ((bf16[32,8,1024]{2,1,0:T(8,128)(2,1)}), bf16[32,8,1024]{2,1,0:T(8,128)(2,1)S(1)}, u32[]{:S(2)}, u32[]{:S(2)}) async-start(bf16[32,8,1024]{2,1,0:T(8,128)(2,1)} %bitcast.6), calls=%async_computation.1 | async-start | bytes 1048576 | tf_op jit(solution)/shard_map/all_to_all | solution.py:202
  123.7 1.2 copy-start.6
  124.9 0.9 copy-start.7
  127.6 17.3 %all-to-all-start.2 = ((bf16[32,32,128]{2,1,0:T(8,128)(2,1)}), bf16[32,32,128]{2,1,0:T(8,128)(2,1)S(1)}, u32[]{:S(2)}, u32[]{:S(2)}) async-start(bf16[32,32,128]{2,1,0:T(8,128)(2,1)} %bitcast.8), calls=%async_computation.2 | async-start | bytes 524288 | tf_op jit(solution)/shard_map/all_to_all | solution.py:202
  136.3 1.0 copy-start.8
  137.2 0.9 copy-start.9

commit v3 on v2

--- a/solution.py
+++ b/solution.py
@@ -86,9 +86,10 @@
     copies = [load(params_hbm, params_ref, sems, 2 * frames)]
     copies += [load(tokens_hbm.at[f], tokens_ref.at[f], sems, f) for f in range(frames)]
     copies += [load(out_grad_hbm.at[f], out_grad_ref.at[f], sems, frames + f) for f in range(frames)]
+    half = rows // 2
     order = one_hot(
-        message_rows((rows, rows), 0, lax.axis_index("yl"), frames, 2)
-        == lax.broadcasted_iota(jnp.int32, (rows, rows), 1)
+        message_rows((half, half), 0, lax.axis_index("yl"), frames, 2)
+        == lax.broadcasted_iota(jnp.int32, (half, half), 1)
     )
     copies[0].wait()
     slots_in, slot_grad = [], []
@@ -103,7 +104,10 @@
         slots_in.append(dot(dispatch.astype(bf16), tokens, ((0,), (0,))).astype(bf16))
         copies[1 + frames + f].wait()
         slot_grad.append(dot(combine.astype(bf16), out_grad_ref[f], ((0,), (0,))).astype(bf16))
-    message_ref[...] = dot(order, jnp.concatenate(slots_in + slot_grad, axis=0)).astype(bf16)
+    part = half // (2 * frames)
+    for i in range(2):
+        value = jnp.concatenate([slots[i * part : (i + 1) * part] for slots in slots_in + slot_grad], axis=0)
+        message_ref[i * half : (i + 1) * half, :] = dot(order, value).astype(bf16)
 
 
 def sort_order(rows, frames, arrays, axis):
@@ -114,15 +118,18 @@
     return (rest // frames) * (kinds * frames) + kind * frames + (rest & (frames - 1))
 
 
-def sort_kernel(frames, message_ref, *out_refs):
-    rows, depth = message_ref.shape
+def sort_kernel(frames, message_ref, _, own_ref, other_ref):
+    half = message_ref.shape[0] // 2
     order = one_hot(
-        sort_order(rows, frames, 2, 0) == lax.broadcasted_iota(jnp.int32, (rows, rows), 1)
-    )
-    out = dot(order, message_ref[...]).astype(bf16)
-    part = rows // len(out_refs)
-    for i, out_ref in enumerate(out_refs):
-        out_ref[...] = out[i * part : (i + 1) * part].reshape(out_ref.shape)
+        sort_order(half, frames, 2, 0) == lax.broadcasted_iota(jnp.int32, (half, half), 1)
+    )
+    part = half // 8
+    for i in range(2):
+        out = dot(order, message_ref[i * half : (i + 1) * half, :]).astype(bf16)
+        for kind in range(8):
+            rel, array, e2 = kind // 4, kind // 2 % 2, kind % 2
+            target = (own_ref, other_ref)[rel]
+            target[array, e2, i * part : (i + 1) * part, :] = out[kind * part : (kind + 1) * part]
 
 
 def unsort_kernel(frames, own_ref, across_ref, back_ref, ahead_ref, message_ref):
@@ -251,7 +258,7 @@
     message, combine_part = lax.optimization_barrier((message, combine_part))
 
     own, other = call(
-        functools.partial(sort_kernel, frames), (shape((2, 2, block, depth), bf16),) * 2, message,
+        functools.partial(sort_kernel, frames), (shape((2, 2, block, depth), bf16),) * 2, message, w_out,
         flops=4 * sort_flops,
     )
     near = [own, to_y(other, 1), to_y(other, -1), to_y(own, 2)]
@@ -297,6 +304,7 @@
         return (near[i] + far[i].astype(f32)).astype(bf16)
 
     back, ahead, across, own = summed(1), summed(2), summed(3), summed(0)
+    own, slot_rows = lax.optimization_barrier((own, slot_rows))
     back, ahead, across = to_y(back, -1), to_y(ahead, 1), to_y(across, 2)
     w_out_grad = jnp.einsum(
         "erh,erd->ehd", active, grad_rows, preferred_element_type=f32
@@ -304,13 +312,12 @@
     w_in_grad = jnp.einsum(
         "erd,erh->edh", slot_rows, pre_grad, preferred_element_type=f32
     ).astype(bf16)
-    own, w_in_grad = lax.optimization_barrier((own, w_in_grad))
+    own, w_in_grad, w_out_grad = lax.optimization_barrier((own, w_in_grad, w_out_grad))
     message = call(
         functools.partial(unsort_kernel, frames), shape((rows, depth), bf16),
         own, across, back, ahead, flops=sort_flops,
     )
     message = exchange(message.reshape(groups, rows // groups, depth)).reshape(rows, depth)
-    message, w_out_grad = lax.optimization_barrier((message, w_out_grad))
 
     slots_in_grad, logits_low, total = call(
         tail_kernel,

time: 170 us -> 165 us (0.971)
  blocking collectives: 23.6 us -> 45.6 us
  waiting for transfers between devices: 58.4 us -> 47 us
  starting transfers between devices: 50.8 us -> 43.5 us
  local copies, waits for them, and re-layouts: 5.89 us -> 0.08 us
    all_to_all x2 -> x3, blocking collectives: 23.6 us -> 45.6 us  [exchange(): return lax.all_to_all(value, axes, split_axis=0, concat_axis=0, tiled=True)]
    all_to_all x3 -> x2, waiting for transfers between devices: 39.8 us -> 30.8 us  [exchange(): return lax.all_to_all(value, axes, split_axis=0, concat_axis=0, tiled=True)]
    all_to_all x3 -> x2, starting transfers between devices: 27 us -> 19.3 us  [exchange(): return lax.all_to_all(value, axes, split_axis=0, concat_axis=0, tiled=True)]
    unnamed x20 -> x12, local copies, waits for them, and re-layouts: 5.84 us -> 0.03 us
    ppermute x5, waiting for transfers between devices: 2.66 us -> 0.01 us  [to_core(): return lax.ppermute(value, 'core', CORE_SWAP)]
  transfers between devices with their start and end apart: 14 -> 13, of which waited for: 7 -> 5; matrix products, arithmetic and copies ran while one was open for 6% -> 5% of each run, Pallas kernels for 3% -> 3%
where the time goes in v3:
time: 165 us; the launch traced here: 164 us
  waiting for transfers between devices  47 us (28%)
  blocking collectives  45.6 us (28%)
  starting transfers between devices  43.5 us (26%)
  Pallas kernels  17.2 us (10%)
  matrix products  8.95 us (5%)
    all_to_all x3, blocking collectives, exchange(): return lax.all_to_all(value, axes, split_axis=0, concat_axis=0, tiled=True)  45.6 us
    all_to_all x2, waiting for transfers between devices, exchange(): return lax.all_to_all(value, axes, split_axis=0, concat_axis=0, tiled=True)  30.8 us
    all_to_all x2, starting transfers between devices, exchange(): return lax.all_to_all(value, axes, split_axis=0, concat_axis=0, tiled=True)  19.3 us
    pallas_call x7, Pallas kernels, call(): pl.pallas_call(kernel, out_shape=out_shape, grid=grid, in_specs=in_specs,...  17.2 us
    ppermute x5, starting transfers between devices, to_core(): return lax.ppermute(value, 'core', CORE_SWAP)  16.4 us
    ppermute x6, waiting for transfers between devices, to_y(): return lax.ppermute(value, Y, [(i, (i + step) % 4) for i in range(4)])  16.3 us
    ppermute x6, starting transfers between devices, to_y(): return lax.ppermute(value, Y, [(i, (i + step) % 4) for i in range(4)])  7.8 us
    dot_general x1, matrix products, shards(): jnp.einsum('erd,erh->edh', slot_rows, pre_grad, preferred_element_type=f32)  3.33 us
  transfers between devices with their start and end apart: 13, of which 5 were waited for; matrix products, arithmetic and copies ran while one was open for 5% of the time, Pallas kernels for 3%

profile of v3, /device:TPU:1, one launch (start us, length us, event | category | flops | bytes accessed | tf_op | source)
XLA Modules:
  0.0 164.4 jit_solution(11885694699017512688)
XLA Ops:
  0.6 4.3 %shard_map.93 = (bf16[512,1024]{1,0:T(8,128)(2,1)}, f32[2,256,128]{2,1,0:T(8,128)}, f32[2,256,128]{2,1,0:T(8,128)}) custom-call(bf16[1024,128]{1,0:T(8,128)(2,1)} %params_ref.1, bf16[2,256,1024]{2,1,0:T(8,128)(2,1)} %tokens_ref.1, bf16[2,256,1024]{2,1,0:T(8,128)(2,1)} %out_grad_hbm.1), custom_call_target="tpu_custom_call" | custom-call | flops 939524096 | bytes 3932160 | tf_op jit(solution)/shard_map/pallas_call | solution.py:49
  4.9 12.0 %all-to-all-start = ((bf16[32,16,1024]{2,1,0:T(8,128)(2,1)}), bf16[32,16,1024]{2,1,0:T(8,128)(2,1)}, u32[]{:S(2)}, u32[]{:S(2)}) async-start(bf16[32,16,1024]{2,1,0:T(8,128)(2,1)} %bitcast.26), calls=%async_computation | async-start | bytes 2097152 | tf_op jit(solution)/shard_map/all_to_all | solution.py:209
  17.0 2.6 %fusion.2.part_ref = f32[2,256,128]{2,1,0:T(8,128)S(1)} fusion(f32[2,256,128]{2,1,0:T(8,128)} %get-tuple-element.34, bf16[2,256,1024]{2,1,0:T(8,128)(2,1)} %out_grad_hbm.1, bf16[2,128,1024]{2,1,0:T(8,128)(2,1)S(1)} %copy-done), kind=kOutput, calls=%fused_computation.4 | convolution fusion | flops 268632704 | bytes 2097152 | tf_op jit(solution)/shard_map/sub | solution.py:256
  19.5 23.6 %all-to-all-done = bf16[32,16,1024]{2,1,0:T(8,128)(2,1)} async-done(((bf16[32,16,1024]{2,1,0:T(8,128)(2,1)}), bf16[32,16,1024]{2,1,0:T(8,128)(2,1)}, u32[]{:S(2)}, u32[]{:S(2)}) %all-to-all-start) | async-done | bytes 1048608 | tf_op jit(solution)/shard_map/all_to_all | solution.py:209
  43.1 1.9 %shard_map.94 = (bf16[2,2,64,1024]{3,2,1,0:T(8,128)(2,1)S(1)}, bf16[2,2,64,1024]{3,2,1,0:T(8,128)(2,1)S(1)}) custom-call(bf16[512,1024]{1,0:T(8,128)(2,1)} %bitcast.1.message_ref, bf16[2,640,1024]{2,1,0:T(8,128)(2,1)S(1)} %copy-done.1), custom_call_target="tpu_custom_call" | custom-call | flops 536870912 | bytes 4718592 | tf_op jit(solution)/shard_map/pallas_call | solution.py:49
  46.4 1.5 collective-permute-start.1
  47.9 1.6 collective-permute-start.2
  49.5 7.5 %collective-permute-done.refs_1_ = bf16[2,2,64,1024]{3,2,1,0:T(8,128)(2,1)S(1)} collective-permute-done((bf16[2,2,64,1024]{3,2,1,0:T(8,128)(2,1)S(1)}, bf16[2,2,64,1024]{3,2,1,0:T(8,128)(2,1)S(1)}, u32[]{:S(2)}, u32[]{:S(2)}) %collective-permute-start) | collective-permute-done | bytes 524320 | tf_op jit(solution)/shard_map/ppermute | solution.py:201
  57.0 5.9 %collective-permute-start.3 = (bf16[2,2,64,1024]{3,2,1,0:T(8,128)(2,1)S(1)}, bf16[2,2,64,1024]{3,2,1,0:T(8,128)(2,1)S(1)}, u32[]{:S(2)}, u32[]{:S(2)}) collective-permute-start(bf16[2,2,64,1024]{3,2,1,0:T(8,128)(2,1)S(1)} %collective-permute-done.refs_1_), channel_id=1, source_target_pairs={{0,64},{64,0},{1,65},{65,1},{2,66},{66,2},{3,67},{67,3},{4,68},{68... | collective-permute-start | bytes 1572872 | tf_op jit(solution)/shard_map/ppermute | solution.py:205
  62.9 8.4 %collective-permute-start.5 = (bf16[2,2,64,1024]{3,2,1,0:T(8,128)(2,1)S(1)}, bf16[2,2,64,1024]{3,2,1,0:T(8,128)(2,1)S(1)}, u32[]{:S(2)}, u32[]{:S(2)}) collective-permute-start(bf16[2,2,64,1024]{3,2,1,0:T(8,128)(2,1)S(1)} %collective-permute-done.1.refs_2_), channel_id=1, source_target_pairs={{0,64},{64,0},{1,65},{65,1},{2,66},{66,2},{3,67},{67,3},{4,68},{68... | collective-permute-start | bytes 1572872 | tf_op jit(solution)/shard_map/ppermute | solution.py:205
  71.3 1.8 %collective-permute-start.6 = (bf16[2,2,64,1024]{3,2,1,0:T(8,128)(2,1)S(1)}, bf16[2,2,64,1024]{3,2,1,0:T(8,128)(2,1)S(1)}, u32[]{:S(2)}, u32[]{:S(2)}) collective-permute-start(bf16[2,2,64,1024]{3,2,1,0:T(8,128)(2,1)S(1)} %collective-permute-done.2.refs_3_), channel_id=1, source_target_pairs={{0,64},{64,0},{1,65},{65,1},{2,66},{66,2},{3,67},{67,3},{4,68},{68... | collective-permute-start | bytes 1572872 | tf_op jit(solution)/shard_map/ppermute | solution.py:205
  73.1 3.8 %shard_map.95 = (bf16[2,512,1024]{2,1,0:T(8,128)(2,1)S(1)}, bf16[2,512,1024]{2,1,0:T(8,128)(2,1)S(1)}, bf16[2,512,640]{2,1,0:T(8,128)(2,1)S(1)}, bf16[2,512,640]{2,1,0:T(8,128)(2,1)S(1)}, f32[4,2,64,1024]{3,2,1,0:T(8,128)S(1)}) custom-call(bf16[2,2,64,1024]{3,2,1,0:T(8,128)(2,1)S(1)} %get-tuple-element.36.refs_0_, ...), custom_call_target="tpu_custom_call" | custom-call | flops 2013265920 | bytes 16252928 | tf_op jit(solution)/shard_map/pallas_call | solution.py:49
  76.9 3.7 %shard_map.96 = (bf16[2,512,1024]{2,1,0:T(8,128)(2,1)S(1)}, bf16[2,512,1024]{2,1,0:T(8,128)(2,1)S(1)}, bf16[2,512,640]{2,1,0:T(8,128)(2,1)S(1)}, bf16[2,512,640]...) custom-call(bf16[2,2,64,1024]{3,2,1,0:T(8,128)(2,1)S(1)} %collective, ...), custom_call_target="tpu_custom_call", output_to_operand_aliasing={{0}: (6, {}), {1}: (7, {}), {2}: (8, {}), {3}: (9, {})} | custom-call | flops 2013265920 | bytes 22020096 | tf_op jit(solution)/shard_map/pallas_call | solution.py:49
  81.0 3.1 %convolution_convert_fusion = bf16[2,640,1024]{2,1,0:T(8,128)(2,1)} fusion(bf16[2,512,640]{2,1,0:T(8,128)(2,1)S(1)} %get-tuple-element.50, bf16[2,512,1024]{2,1,0:T(8,128)(2,1)S(1)} %get-tuple-element.51), kind=kOutput, calls=%fused_computation.1 | convolution fusion | flops 1343488000 | bytes 6029312 | tf_op jit(solution)/shard_map/erh,erd->ehd/dot_general | solution.py:309
  85.3 1.8 %collective-permute-start.9 = (bf16[2,64,1024]{2,1,0:T(8,128)(2,1)S(1)}, bf16[2,64,1024]{2,1,0:T(8,128)(2,1)S(1)}, u32[]{:S(2)}, u32[]{:S(2)}) collective-permute-start(bf16[2,64,1024]{2,1,0:T(8,128)(2,1)S(1)} %get-tuple-element.63), channel_id=1, source_target_pairs={{0,129},{1,0},{128,1},{129,128},{2,131},{3,2},{130,3},{131,130},{4... | collective-permute-start | bytes 786440 | tf_op jit(solution)/shard_map/ppermute | solution.py:201
  87.7 3.3 %convolution_convert_fusion.1 = bf16[2,1024,640]{2,1,0:T(8,128)(2,1)} fusion(bf16[2,512,1024]{2,1,0:T(8,128)(2,1)S(1)} %get-tuple-element.48, bf16[2,512,640]{2,1,0:T(8,128)(2,1)S(1)} %get-tuple-element.49), kind=kOutput, calls=%fused_computation.2 | convolution fusion | flops 1343488000 | bytes 6029312 | tf_op jit(solution)/shard_map/erd,erh->edh/dot_general | solution.py:312
  91.1 2.0 %collective-permute-done.10.ahead_ref = bf16[2,64,1024]{2,1,0:T(8,128)(2,1)S(1)} collective-permute-done((bf16[2,64,1024]{2,1,0:T(8,128)(2,1)S(1)}, bf16[2,64,1024]{2,1,0:T(8,128)(2,1)S(1)}, u32[]{:S(2)}, u32[]{:S(2)}) %collective-permute-start.10) | collective-permute-done | bytes 262176 | tf_op jit(solution)/shard_map/ppermute | solution.py:201
  93.0 6.7 %collective-permute-done.8.across_ref = bf16[2,64,1024]{2,1,0:T(8,128)(2,1)S(1)} collective-permute-done((bf16[2,64,1024]{2,1,0:T(8,128)(2,1)S(1)}, bf16[2,64,1024]{2,1,0:T(8,128)(2,1)S(1)}, u32[]{:S(2)}, u32[]{:S(2)}) %collective-permute-start.8) | collective-permute-done | bytes 262176 | tf_op jit(solution)/shard_map/ppermute | solution.py:201
  100.1 21.9 %all_to_all.25 = bf16[32,8,1024]{2,1,0:T(8,128)(2,1)S(1)} all-to-all(bf16[32,8,1024]{2,1,0:T(8,128)(2,1)S(1)} %bitcast.24), channel_id=1, replica_groups=mesh['yh'=2,'core'=2,'z'=8,'x'=4,'yl'=2] {'z','x'}, dimensions={0} | all-to-all | bytes 1048576 | tf_op jit(solution)/shard_map/all_to_all | solution.py:209
  122.0 1.8 %shard_map.98 = (bf16[2,128,1024]{2,1,0:T(8,128)(2,1)S(1)}, bf16[2,256,128]{2,1,0:T(8,128)(2,1)S(1)}, bf16[1024,128]{1,0:T(8,128)(2,1)}) custom-call(bf16[256,1024]{1,0:T(8,128)(2,1)S(1)} %bitcast.25, bf16[2,256,1024]{2,1,0:T(8,128)(2,1)S(1)} %copy-done.3, f32[2,256,128]{2,1,0:T(8,128)S(1)} %copy-done.4, f32[2,256,128]{2,1,0:T(8,128)S(1)} %fusion.2.part_ref), custom_call_target="tpu_custom_call" | custom-call | flops 402653184 | bytes 3014656 | tf_op jit(solution)/shard_map/pallas_call | solution.py:49
  123.8 7.3 %all-to-all-start.2 = ((bf16[32,32,128]{2,1,0:T(8,128)(2,1)}), bf16[32,32,128]{2,1,0:T(8,128)(2,1)S(1)}, u32[]{:S(2)}, u32[]{:S(2)}) async-start(bf16[32,32,128]{2,1,0:T(8,128)(2,1)} %bitcast.8), calls=%async_computation.2 | async-start | bytes 524288 | tf_op jit(solution)/shard_map/all_to_all | solution.py:209
  132.6 7.2 %all-to-all-done.2 = bf16[32,32,128]{2,1,0:T(8,128)(2,1)S(1)} async-done(((bf16[32,32,128]{2,1,0:T(8,128)(2,1)}), bf16[32,32,128]{2,1,0:T(8,128)(2,1)S(1)}, u32[]{:S(2)}, u32[]{:S(2)}) %all-to-all-start.2) | async-done | bytes 262176 | tf_op jit(solution)/shard_map/all_to_all | solution.py:209
  139.8 9.6 %all_to_all.26 = bf16[8,32,128]{2,1,0:T(8,128)(2,1)S(1)} all-to-all(bf16[8,32,128]{2,1,0:T(8,128)(2,1)S(1)} %broadcast_in_dim.4), channel_id=1, replica_groups=mesh['yh'=2,'core'=2,'z'=8,'x'=4,'yl'=2] {'z'}, dimensions={0} | all-to-all | bytes 131072 | tf_op jit(solution)/shard_map/all_to_all | solution.py:209
  149.5 14.1 %all_to_all.27 = bf16[32,32,128]{2,1,0:T(8,128)(2,1)S(1)} all-to-all(bf16[32,32,128]{2,1,0:T(8,128)(2,1)S(1)} %broadcast_in_dim.5), channel_id=1, replica_groups=mesh['yh'=2,'core'=2,'z'=8,'x'=4,'yl'=2] {'yh','core','x','yl'}, dimensions={0} | all-to-all | bytes 524288 | tf_op jit(solution)/shard_map/all_to_all | solution.py:209
  (33 shorter events, 6.4 us)
Async XLA Ops:
  0.6 16.3 %copy-start = (bf16[2,128,1024]{2,1,0:T(8,128)(2,1)S(1)}, bf16[2,128,1024]{2,1,0:T(8,128)(2,1)}, u32[]{:S(2)}) copy-start(bf16[2,128,1024]{2,1,0:T(8,128)(2,1)} %param.10) | copy-start | bytes 1572868
  4.9 38.2 %all-to-all-start = ((bf16[32,16,1024]{2,1,0:T(8,128)(2,1)}), bf16[32,16,1024]{2,1,0:T(8,128)(2,1)}, u32[]{:S(2)}, u32[]{:S(2)}) async-start(bf16[32,16,1024]{2,1,0:T(8,128)(2,1)} %bitcast.26), calls=%async_computation | async-start | bytes 2097152 | tf_op jit(solution)/shard_map/all_to_all | solution.py:209
  16.9 26.2 %copy-start.1 = (bf16[2,640,1024]{2,1,0:T(8,128)(2,1)S(1)}, bf16[2,640,1024]{2,1,0:T(8,128)(2,1)}, u32[]{:S(2)}) copy-start(bf16[2,640,1024]{2,1,0:T(8,128)(2,1)} %refs_5_.3) | copy-start | bytes 7864324
  43.1 30.0 %copy-start.2 = (bf16[2,1024,640]{2,1,0:T(8,128)(2,1)S(1)}, bf16[2,1024,640]{2,1,0:T(8,128)(2,1)}, u32[]{:S(2)}) copy-start(bf16[2,1024,640]{2,1,0:T(8,128)(2,1)} %refs_4_.3) | copy-start | bytes 7864324
  45.0 12.0 %collective-permute-start = (bf16[2,2,64,1024]{3,2,1,0:T(8,128)(2,1)S(1)}, bf16[2,2,64,1024]{3,2,1,0:T(8,128)(2,1)S(1)}, u32[]{:S(2)}, u32[]{:S(2)}) collective-permute-start(bf16[2,2,64,1024]{3,2,1,0:T(8,128)(2,1)S(1)} %get-tuple-element.37), channel_id=1, source_target_pairs={{0,1},{1,128},{128,129},{129,0},{2,3},{3,130},{130,131},{131,2},{4... | collective-permute-start | bytes 1572872 | tf_op jit(solution)/shard_map/ppermute | solution.py:201
  46.4 16.5 %collective-permute-start.1 = (bf16[2,2,64,1024]{3,2,1,0:T(8,128)(2,1)S(1)}, bf16[2,2,64,1024]{3,2,1,0:T(8,128)(2,1)S(1)}, u32[]{:S(2)}, u32[]{:S(2)}) collective-permute-start(bf16[2,2,64,1024]{3,2,1,0:T(8,128)(2,1)S(1)} %get-tuple-element.37), channel_id=1, source_target_pairs={{0,129},{1,0},{128,1},{129,128},{2,131},{3,2},{130,3},{131,130},{4... | collective-permute-start | bytes 1572872 | tf_op jit(solution)/shard_map/ppermute | solution.py:201
  47.9 23.4 %collective-permute-start.2 = (bf16[2,2,64,1024]{3,2,1,0:T(8,128)(2,1)S(1)}, bf16[2,2,64,1024]{3,2,1,0:T(8,128)(2,1)S(1)}, u32[]{:S(2)}, u32[]{:S(2)}) collective-permute-start(bf16[2,2,64,1024]{3,2,1,0:T(8,128)(2,1)S(1)} %get-tuple-element.36.refs_0_), channel_id=1, source_target_pairs={{0,128},{1,129},{128,0},{129,1},{2,130},{3,131},{130,2},{131,3},{4... | collective-permute-start | bytes 1572872 | tf_op jit(solution)/shard_map/ppermute | solution.py:201
  57.0 19.9 %collective-permute-start.3 = (bf16[2,2,64,1024]{3,2,1,0:T(8,128)(2,1)S(1)}, bf16[2,2,64,1024]{3,2,1,0:T(8,128)(2,1)S(1)}, u32[]{:S(2)}, u32[]{:S(2)}) collective-permute-start(bf16[2,2,64,1024]{3,2,1,0:T(8,128)(2,1)S(1)} %collective-permute-done.refs_1_), channel_id=1, source_target_pairs={{0,64},{64,0},{1,65},{65,1},{2,66},{66,2},{3,67},{67,3},{4,68},{68... | collective-permute-start | bytes 1572872 | tf_op jit(solution)/shard_map/ppermute | solution.py:205
  62.9 14.0 %collective-permute-start.4 = (bf16[2,2,64,1024]{3,2,1,0:T(8,128)(2,1)S(1)}, bf16[2,2,64,1024]{3,2,1,0:T(8,128)(2,1)S(1)}, u32[]{:S(2)}, u32[]{:S(2)}) collective-permute-start(bf16[2,2,64,1024]{3,2,1,0:T(8,128)(2,1)S(1)} %get-tuple-element.36.refs_0_), channel_id=1, source_target_pairs={{0,64},{64,0},{1,65},{65,1},{2,66},{66,2},{3,67},{67,3},{4,68},{68... | collective-permute-start | bytes 1572872 | tf_op jit(solution)/shard_map/ppermute | solution.py:205
  62.9 14.0 %collective-permute-start.5 = (bf16[2,2,64,1024]{3,2,1,0:T(8,128)(2,1)S(1)}, bf16[2,2,64,1024]{3,2,1,0:T(8,128)(2,1)S(1)}, u32[]{:S(2)}, u32[]{:S(2)}) collective-permute-start(bf16[2,2,64,1024]{3,2,1,0:T(8,128)(2,1)S(1)} %collective-permute-done.1.refs_2_), channel_id=1, source_target_pairs={{0,64},{64,0},{1,65},{65,1},{2,66},{66,2},{3,67},{67,3},{4,68},{68... | collective-permute-start | bytes 1572872 | tf_op jit(solution)/shard_map/ppermute | solution.py:205
  71.3 5.6 %collective-permute-start.6 = (bf16[2,2,64,1024]{3,2,1,0:T(8,128)(2,1)S(1)}, bf16[2,2,64,1024]{3,2,1,0:T(8,128)(2,1)S(1)}, u32[]{:S(2)}, u32[]{:S(2)}) collective-permute-start(bf16[2,2,64,1024]{3,2,1,0:T(8,128)(2,1)S(1)} %collective-permute-done.2.refs_3_), channel_id=1, source_target_pairs={{0,64},{64,0},{1,65},{65,1},{2,66},{66,2},{3,67},{67,3},{4,68},{68... | collective-permute-start | bytes 1572872 | tf_op jit(solution)/shard_map/ppermute | solution.py:205
  80.7 3.3 %collective-permute-start.7 = (bf16[4,2,64,1024]{3,2,1,0:T(8,128)(2,1)S(1)}, bf16[4,2,64,1024]{3,2,1,0:T(8,128)(2,1)S(1)}, u32[]{:S(2)}, u32[]{:S(2)}) collective-permute-start(bf16[4,2,64,1024]{3,2,1,0:T(8,128)(2,1)S(1)} %get-tuple-element.45), channel_id=1, source_target_pairs={{0,64},{64,0},{1,65},{65,1},{2,66},{66,2},{3,67},{67,3},{4,68},{68... | collective-permute-start | bytes 3145736 | tf_op jit(solution)/shard_map/ppermute | solution.py:205
  84.4 8.7 %collective-permute-start.10 = (bf16[2,64,1024]{2,1,0:T(8,128)(2,1)S(1)}, bf16[2,64,1024]{2,1,0:T(8,128)(2,1)S(1)}, u32[]{:S(2)}, u32[]{:S(2)}) collective-permute-start(bf16[2,64,1024]{2,1,0:T(8,128)(2,1)S(1)} %get-tuple-element.62), channel_id=1, source_target_pairs={{0,1},{1,128},{128,129},{129,0},{2,3},{3,130},{130,131},{131,2},{4... | collective-permute-start | bytes 786440 | tf_op jit(solution)/shard_map/ppermute | solution.py:201
  85.3 7.7 %collective-permute-start.9 = (bf16[2,64,1024]{2,1,0:T(8,128)(2,1)S(1)}, bf16[2,64,1024]{2,1,0:T(8,128)(2,1)S(1)}, u32[]{:S(2)}, u32[]{:S(2)}) collective-permute-start(bf16[2,64,1024]{2,1,0:T(8,128)(2,1)S(1)} %get-tuple-element.63), channel_id=1, source_target_pairs={{0,129},{1,0},{128,1},{129,128},{2,131},{3,2},{130,3},{131,130},{4... | collective-permute-start | bytes 786440 | tf_op jit(solution)/shard_map/ppermute | solution.py:201
  87.1 12.6 %collective-permute-start.8 = (bf16[2,64,1024]{2,1,0:T(8,128)(2,1)S(1)}, bf16[2,64,1024]{2,1,0:T(8,128)(2,1)S(1)}, u32[]{:S(2)}, u32[]{:S(2)}) collective-permute-start(bf16[2,64,1024]{2,1,0:T(8,128)(2,1)S(1)} %get-tuple-element.64), channel_id=1, source_target_pairs={{0,128},{1,129},{128,0},{129,1},{2,130},{3,131},{130,2},{131,3},{4... | collective-permute-start | bytes 786440 | tf_op jit(solution)/shard_map/ppermute | solution.py:201
  91.1 30.9 %copy-start.3 = (bf16[2,256,1024]{2,1,0:T(8,128)(2,1)S(1)}, bf16[2,256,1024]{2,1,0:T(8,128)(2,1)}, u32[]{:S(2)}) copy-start(bf16[2,256,1024]{2,1,0:T(8,128)(2,1)} %tokens_ref.1) | copy-start | bytes 3145732
  91.1 30.9 %copy-start.4 = (f32[2,256,128]{2,1,0:T(8,128)S(1)}, f32[2,256,128]{2,1,0:T(8,128)}, u32[]{:S(2)}) copy-start(f32[2,256,128]{2,1,0:T(8,128)} %get-tuple-element.53.dispatch_ref) | copy-start | bytes 786436
  100.1 30.9 %copy-start.5 = (bf16[1024,128]{1,0:T(8,128)(2,1)S(1)}, bf16[1024,128]{1,0:T(8,128)(2,1)}, u32[]{:S(2)}) copy-start(bf16[1024,128]{1,0:T(8,128)(2,1)} %params_ref.1) | copy-start | bytes 786436
  123.8 15.9 %all-to-all-start.2 = ((bf16[32,32,128]{2,1,0:T(8,128)(2,1)}), bf16[32,32,128]{2,1,0:T(8,128)(2,1)S(1)}, u32[]{:S(2)}, u32[]{:S(2)}) async-start(bf16[32,32,128]{2,1,0:T(8,128)(2,1)} %bitcast.8), calls=%async_computation.2 | async-start | bytes 524288 | tf_op jit(solution)/shard_map/all_to_all | solution.py:209

commit v4 on v3

--- a/solution.py
+++ b/solution.py
@@ -147,14 +147,14 @@
 
 
 def expert_kernel(count, *refs):
-    pieces, w_in_ref, w_out_ref = refs[:count], refs[count], refs[count + 1]
+    pieces, w_in_ref, w_out_back_ref = refs[:count], refs[count], refs[count + 1]
     rows_ref, grads_ref, active_ref, pre_ref, partial_ref = refs[-5:]
     rows = jnp.concatenate([piece[0, 0] for piece in pieces], axis=0)
     grads = jnp.concatenate([piece[1, 0] for piece in pieces], axis=0)
     rows_ref[0] = rows
     grads_ref[0] = grads
     hidden = dot(rows, w_in_ref[0])
-    act_grad = dot(grads, w_out_ref[0], ((1,), (1,)))
+    act_grad = dot(grads, w_out_back_ref[0])
     cdf = 0.5 * (1.0 + lax.erf(hidden * inv_root_two))
     dens = jnp.exp(-0.5 * hidden * hidden) * inv_root_tau
     active_ref[0] = (hidden * cdf).astype(bf16)
@@ -255,10 +255,11 @@
     combine_part = combine * (
         combine_grad - jnp.sum(combine * combine_grad, axis=2, keepdims=True)
     )
-    message, combine_part = lax.optimization_barrier((message, combine_part))
+    w_out_back = jnp.swapaxes(w_out, 1, 2)
+    message, combine_part, w_out_back = lax.optimization_barrier((message, combine_part, w_out_back))
 
     own, other = call(
-        functools.partial(sort_kernel, frames), (shape((2, 2, block, depth), bf16),) * 2, message, w_out,
+        functools.partial(sort_kernel, frames), (shape((2, 2, block, depth), bf16),) * 2, message, w_out_back,
         flops=4 * sort_flops,
     )
     near = [own, to_y(other, 1), to_y(other, -1), to_y(own, 2)]
@@ -266,7 +267,6 @@
 
     piece = pl.BlockSpec((2, 1, block, depth), lambda e: (0, e, 0, 0))
     w_in_spec = pl.BlockSpec((1, depth, hidden_size), lambda e: (e, 0, 0))
-    w_out_spec = pl.BlockSpec((1, hidden_size, depth), lambda e: (e, 0, 0))
     matmul_flops = 2 * 2 * 4 * block * depth * hidden_size
 
     def expert_half(half, pieces, filled):
@@ -281,9 +281,9 @@
                 shape((2, 8 * block, hidden_size), bf16),
                 shape((4, 2, block, depth), bf16 if half else f32),
             ),
-            *pieces, w_in, w_out, *filled,
+            *pieces, w_in, w_out_back, *filled,
             grid=(2,),
-            in_specs=[piece] * 4 + [w_in_spec, w_out_spec] + [ANY] * len(filled),
+            in_specs=[piece] * 4 + [w_in_spec, w_in_spec] + [ANY] * len(filled),
             out_specs=(
                 rows_spec,
                 rows_spec,
@@ -304,7 +304,7 @@
         return (near[i] + far[i].astype(f32)).astype(bf16)
 
     back, ahead, across, own = summed(1), summed(2), summed(3), summed(0)
-    own, slot_rows = lax.optimization_barrier((own, slot_rows))
+    own, slot_rows, active = lax.optimization_barrier((own, slot_rows, active))
     back, ahead, across = to_y(back, -1), to_y(ahead, 1), to_y(across, 2)
     w_out_grad = jnp.einsum(
         "erh,erd->ehd", active, grad_rows, preferred_element_type=f32

time: 165 us -> 164 us (level)
  waiting for transfers between devices: 47 us -> 43.2 us
  local copies, waits for them, and re-layouts: 0.08 us -> 3.22 us
    ppermute x6, waiting for transfers between devices: 16.3 us -> 12.8 us  [to_y(): return lax.ppermute(value, Y, [(i, (i + step) % 4) for i in range(4)])]
    unnamed x12 -> x11, local copies, waits for them, and re-layouts: 0.03 us -> 3.17 us
    all_to_all x2, waiting for transfers between devices: 30.8 us -> 27.8 us  [exchange(): return lax.all_to_all(value, axes, split_axis=0, concat_axis=0, tiled=True)]
    ppermute x5, waiting for transfers between devices: 0.01 us -> 2.66 us  [to_core(): return lax.ppermute(value, 'core', CORE_SWAP)]
  transfers between devices with their start and end apart: 13 -> 13, of which waited for: 5 -> 5; matrix products, arithmetic and copies ran while one was open for 5% -> 7% of each run, Pallas kernels for 3% -> 3%
where the time goes in v4:
time: 164 us; the launch traced here: 163 us
  blocking collectives  45.3 us (28%)
  starting transfers between devices  44.3 us (27%)
  waiting for transfers between devices  43.2 us (26%)
  Pallas kernels  16.2 us (10%)
  matrix products  8.83 us (5%)
  local copies, waits for them, and re-layouts  3.22 us (2%)
    all_to_all x3, blocking collectives, exchange(): return lax.all_to_all(value, axes, split_axis=0, concat_axis=0, tiled=True)  45.3 us
    all_to_all x2, waiting for transfers between devices, exchange(): return lax.all_to_all(value, axes, split_axis=0, concat_axis=0, tiled=True)  27.8 us
    all_to_all x2, starting transfers between devices, exchange(): return lax.all_to_all(value, axes, split_axis=0, concat_axis=0, tiled=True)  20.7 us
    ppermute x5, starting transfers between devices, to_core(): return lax.ppermute(value, 'core', CORE_SWAP)  16.2 us
    pallas_call x7, Pallas kernels, call(): pl.pallas_call(kernel, out_shape=out_shape, grid=grid, in_specs=in_specs,...  16.2 us
    ppermute x6, waiting for transfers between devices, to_y(): return lax.ppermute(value, Y, [(i, (i + step) % 4) for i in range(4)])  12.8 us
    ppermute x6, starting transfers between devices, to_y(): return lax.ppermute(value, Y, [(i, (i + step) % 4) for i in range(4)])  7.45 us
    dot_general x1, matrix products, shards(): jnp.einsum('erd,erh->edh', slot_rows, pre_grad, preferred_element_type=f32)  3.33 us
  transfers between devices with their start and end apart: 13, of which 5 were waited for; matrix products, arithmetic and copies ran while one was open for 7% of the time, Pallas kernels for 3%

profile of v4, /device:TPU:1, one launch (start us, length us, event | category | flops | bytes accessed | tf_op | source)
XLA Modules:
  0.0 163.1 jit_solution(13976504675531783934)
XLA Ops:
  0.6 4.3 %shard_map.93 = (bf16[512,1024]{1,0:T(8,128)(2,1)}, f32[2,256,128]{2,1,0:T(8,128)}, f32[2,256,128]{2,1,0:T(8,128)}) custom-call(bf16[1024,128]{1,0:T(8,128)(2,1)} %params_ref.1, bf16[2,256,1024]{2,1,0:T(8,128)(2,1)} %tokens_ref.1, bf16[2,256,1024]{2,1,0:T(8,128)(2,1)} %out_grad_hbm.1), custom_call_target="tpu_custom_call" | custom-call | flops 939524096 | bytes 3932160 | tf_op jit(solution)/shard_map/pallas_call | solution.py:49
  4.9 12.0 %all-to-all-start = ((bf16[32,16,1024]{2,1,0:T(8,128)(2,1)}), bf16[32,16,1024]{2,1,0:T(8,128)(2,1)}, u32[]{:S(2)}, u32[]{:S(2)}) async-start(bf16[32,16,1024]{2,1,0:T(8,128)(2,1)} %bitcast.30), calls=%async_computation | async-start | bytes 2097152 | tf_op jit(solution)/shard_map/all_to_all | solution.py:209
  16.9 3.1 %copy.21 = bf16[2,640,1024]{1,2,0:T(8,128)(2,1)S(1)} copy(bf16[2,640,1024]{2,1,0:T(8,128)(2,1)} %param.9) | data formatting | bytes 5242880 | tf_op args[3]
  20.1 2.4 %fusion.2.part_ref = f32[2,256,128]{2,1,0:T(8,128)S(1)} fusion(f32[2,256,128]{2,1,0:T(8,128)} %get-tuple-element.36, bf16[2,256,1024]{2,1,0:T(8,128)(2,1)} %out_grad_hbm.1, bf16[2,128,1024]{2,1,0:T(8,128)(2,1)S(1)} %copy-done), kind=kOutput, calls=%fused_computation.4 | convolution fusion | flops 268632704 | bytes 2097152 | tf_op jit(solution)/shard_map/sub | solution.py:256
  22.5 20.6 %all-to-all-done = bf16[32,16,1024]{2,1,0:T(8,128)(2,1)} async-done(((bf16[32,16,1024]{2,1,0:T(8,128)(2,1)}), bf16[32,16,1024]{2,1,0:T(8,128)(2,1)}, u32[]{:S(2)}, u32[]{:S(2)}) %all-to-all-start) | async-done | bytes 1048608 | tf_op jit(solution)/shard_map/all_to_all | solution.py:209
  43.1 1.9 %shard_map.94 = (bf16[2,2,64,1024]{3,2,1,0:T(8,128)(2,1)S(1)}, bf16[2,2,64,1024]{3,2,1,0:T(8,128)(2,1)S(1)}) custom-call(bf16[512,1024]{1,0:T(8,128)(2,1)} %bitcast.1.message_ref, bf16[2,1024,640]{2,1,0:T(8,128)(2,1)S(1)} %bitcast.25), custom_call_target="tpu_custom_call" | custom-call | flops 536870912 | bytes 4718592 | tf_op jit(solution)/shard_map/pallas_call | solution.py:49
  47.9 1.6 collective-permute-start.2
  49.5 7.5 %collective-permute-done.refs_1_ = bf16[2,2,64,1024]{3,2,1,0:T(8,128)(2,1)S(1)} collective-permute-done((bf16[2,2,64,1024]{3,2,1,0:T(8,128)(2,1)S(1)}, bf16[2,2,64,1024]{3,2,1,0:T(8,128)(2,1)S(1)}, u32[]{:S(2)}, u32[]{:S(2)}) %collective-permute-start) | collective-permute-done | bytes 524320 | tf_op jit(solution)/shard_map/ppermute | solution.py:201
  57.0 5.9 %collective-permute-start.3 = (bf16[2,2,64,1024]{3,2,1,0:T(8,128)(2,1)S(1)}, bf16[2,2,64,1024]{3,2,1,0:T(8,128)(2,1)S(1)}, u32[]{:S(2)}, u32[]{:S(2)}) collective-permute-start(bf16[2,2,64,1024]{3,2,1,0:T(8,128)(2,1)S(1)} %collective-permute-done.refs_1_), channel_id=1, source_target_pairs={{0,64},{64,0},{1,65},{65,1},{2,66},{66,2},{3,67},{67,3},{4,68},{68... | collective-permute-start | bytes 1572872 | tf_op jit(solution)/shard_map/ppermute | solution.py:205
  62.9 8.4 %collective-permute-start.5 = (bf16[2,2,64,1024]{3,2,1,0:T(8,128)(2,1)S(1)}, bf16[2,2,64,1024]{3,2,1,0:T(8,128)(2,1)S(1)}, u32[]{:S(2)}, u32[]{:S(2)}) collective-permute-start(bf16[2,2,64,1024]{3,2,1,0:T(8,128)(2,1)S(1)} %collective-permute-done.1.refs_2_), channel_id=1, source_target_pairs={{0,64},{64,0},{1,65},{65,1},{2,66},{66,2},{3,67},{67,3},{4,68},{68... | collective-permute-start | bytes 1572872 | tf_op jit(solution)/shard_map/ppermute | solution.py:205
  71.3 1.8 %collective-permute-start.6 = (bf16[2,2,64,1024]{3,2,1,0:T(8,128)(2,1)S(1)}, bf16[2,2,64,1024]{3,2,1,0:T(8,128)(2,1)S(1)}, u32[]{:S(2)}, u32[]{:S(2)}) collective-permute-start(bf16[2,2,64,1024]{3,2,1,0:T(8,128)(2,1)S(1)} %collective-permute-done.2.refs_3_), channel_id=1, source_target_pairs={{0,64},{64,0},{1,65},{65,1},{2,66},{66,2},{3,67},{67,3},{4,68},{68... | collective-permute-start | bytes 1572872 | tf_op jit(solution)/shard_map/ppermute | solution.py:205
  73.1 3.2 %shard_map.95 = (bf16[2,512,1024]{2,1,0:T(8,128)(2,1)S(1)}, bf16[2,512,1024]{2,1,0:T(8,128)(2,1)S(1)}, bf16[2,512,640]{2,1,0:T(8,128)(2,1)S(1)}, bf16[2,512,640]{2,1,0:T(8,128)(2,1)S(1)}, f32[4,2,64,1024]{3,2,1,0:T(8,128)S(1)}) custom-call(bf16[2,2,64,1024]{3,2,1,0:T(8,128)(2,1)S(1)} %get-tuple-element.39.refs_0_, ...), custom_call_target="tpu_custom_call" | custom-call | flops 2013265920 | bytes 16252928 | tf_op jit(solution)/shard_map/pallas_call | solution.py:49
  76.4 3.2 %shard_map.96 = (bf16[2,512,1024]{2,1,0:T(8,128)(2,1)S(1)}, bf16[2,512,1024]{2,1,0:T(8,128)(2,1)S(1)}, bf16[2,512,640]{2,1,0:T(8,128)(2,1)S(1)}, bf16[2,512,640]...) custom-call(bf16[2,2,64,1024]{3,2,1,0:T(8,128)(2,1)S(1)} %collective, ...), custom_call_target="tpu_custom_call", output_to_operand_aliasing={{0}: (6, {}), {1}: (7, {}), {2}: (8, {}), {3}: (9, {})} | custom-call | flops 2013265920 | bytes 22020096 | tf_op jit(solution)/shard_map/pallas_call | solution.py:49
  79.7 2.6 %collective-permute-done.7 = bf16[4,2,64,1024]{3,2,1,0:T(8,128)(2,1)S(1)} collective-permute-done((bf16[4,2,64,1024]{3,2,1,0:T(8,128)(2,1)S(1)}, bf16[4,2,64,1024]{3,2,1,0:T(8,128)(2,1)S(1)}, u32[]{:S(2)}, u32[]{:S(2)}) %collective-permute-start.7) | collective-permute-done | bytes 1048608 | tf_op jit(solution)/shard_map/ppermute | solution.py:205
  83.7 1.8 %collective-permute-start.9 = (bf16[2,64,1024]{2,1,0:T(8,128)(2,1)S(1)}, bf16[2,64,1024]{2,1,0:T(8,128)(2,1)S(1)}, u32[]{:S(2)}, u32[]{:S(2)}) collective-permute-start(bf16[2,64,1024]{2,1,0:T(8,128)(2,1)S(1)} %get-tuple-element.67), channel_id=1, source_target_pairs={{0,129},{1,0},{128,1},{129,128},{2,131},{3,2},{130,3},{131,130},{4... | collective-permute-start | bytes 786440 | tf_op jit(solution)/shard_map/ppermute | solution.py:201
  85.7 3.1 %convolution_convert_fusion = bf16[2,640,1024]{2,1,0:T(8,128)(2,1)} fusion(bf16[2,512,640]{2,1,0:T(8,128)(2,1)S(1)} %get-tuple-element.54, bf16[2,512,1024]{2,1,0:T(8,128)(2,1)S(1)} %get-tuple-element.55), kind=kOutput, calls=%fused_computation.1 | convolution fusion | flops 1343488000 | bytes 6029312 | tf_op jit(solution)/shard_map/erh,erd->ehd/dot_general | solution.py:309
  88.8 3.3 %convolution_convert_fusion.1 = bf16[2,1024,640]{2,1,0:T(8,128)(2,1)} fusion(bf16[2,512,1024]{2,1,0:T(8,128)(2,1)S(1)} %get-tuple-element.52, bf16[2,512,640]{2,1,0:T(8,128)(2,1)S(1)} %get-tuple-element.53), kind=kOutput, calls=%fused_computation.2 | convolution fusion | flops 1343488000 | bytes 6029312 | tf_op jit(solution)/shard_map/erd,erh->edh/dot_general | solution.py:312
  92.1 5.2 %collective-permute-done.8.across_ref = bf16[2,64,1024]{2,1,0:T(8,128)(2,1)S(1)} collective-permute-done((bf16[2,64,1024]{2,1,0:T(8,128)(2,1)S(1)}, bf16[2,64,1024]{2,1,0:T(8,128)(2,1)S(1)}, u32[]{:S(2)}, u32[]{:S(2)}) %collective-permute-start.8) | collective-permute-done | bytes 262176 | tf_op jit(solution)/shard_map/ppermute | solution.py:201
  97.8 21.6 %all_to_all.25 = bf16[32,8,1024]{2,1,0:T(8,128)(2,1)S(1)} all-to-all(bf16[32,8,1024]{2,1,0:T(8,128)(2,1)S(1)} %bitcast.28), channel_id=1, replica_groups=mesh['yh'=2,'core'=2,'z'=8,'x'=4,'yl'=2] {'z','x'}, dimensions={0} | all-to-all | bytes 1048576 | tf_op jit(solution)/shard_map/all_to_all | solution.py:209
  119.4 1.8 %shard_map.98 = (bf16[2,128,1024]{2,1,0:T(8,128)(2,1)S(1)}, bf16[2,256,128]{2,1,0:T(8,128)(2,1)S(1)}, bf16[1024,128]{1,0:T(8,128)(2,1)}) custom-call(bf16[256,1024]{1,0:T(8,128)(2,1)S(1)} %bitcast.29, bf16[2,256,1024]{2,1,0:T(8,128)(2,1)S(1)} %copy-done.2, f32[2,256,128]{2,1,0:T(8,128)S(1)} %copy-done.3, f32[2,256,128]{2,1,0:T(8,128)S(1)} %fusion.2.part_ref), custom_call_target="tpu_custom_call" | custom-call | flops 402653184 | bytes 3014656 | tf_op jit(solution)/shard_map/pallas_call | solution.py:49
  121.2 8.7 %all-to-all-start.2 = ((bf16[32,32,128]{2,1,0:T(8,128)(2,1)}), bf16[32,32,128]{2,1,0:T(8,128)(2,1)S(1)}, u32[]{:S(2)}, u32[]{:S(2)}) async-start(bf16[32,32,128]{2,1,0:T(8,128)(2,1)} %bitcast.9), calls=%async_computation.2 | async-start | bytes 524288 | tf_op jit(solution)/shard_map/all_to_all | solution.py:209
  131.3 7.2 %all-to-all-done.2 = bf16[32,32,128]{2,1,0:T(8,128)(2,1)S(1)} async-done(((bf16[32,32,128]{2,1,0:T(8,128)(2,1)}), bf16[32,32,128]{2,1,0:T(8,128)(2,1)S(1)}, u32[]{:S(2)}, u32[]{:S(2)}) %all-to-all-start.2) | async-done | bytes 262176 | tf_op jit(solution)/shard_map/all_to_all | solution.py:209
  138.5 9.6 %all_to_all.26 = bf16[8,32,128]{2,1,0:T(8,128)(2,1)S(1)} all-to-all(bf16[8,32,128]{2,1,0:T(8,128)(2,1)S(1)} %broadcast_in_dim.4), channel_id=1, replica_groups=mesh['yh'=2,'core'=2,'z'=8,'x'=4,'yl'=2] {'z'}, dimensions={0} | all-to-all | bytes 131072 | tf_op jit(solution)/shard_map/all_to_all | solution.py:209
  148.2 14.0 %all_to_all.27 = bf16[32,32,128]{2,1,0:T(8,128)(2,1)S(1)} all-to-all(bf16[32,32,128]{2,1,0:T(8,128)(2,1)S(1)} %broadcast_in_dim.5), channel_id=1, replica_groups=mesh['yh'=2,'core'=2,'z'=8,'x'=4,'yl'=2] {'yh','core','x','yl'}, dimensions={0} | all-to-all | bytes 524288 | tf_op jit(solution)/shard_map/all_to_all | solution.py:209
  (32 shorter events, 7.3 us)
Async XLA Ops:
  0.6 19.5 %copy-start = (bf16[2,128,1024]{2,1,0:T(8,128)(2,1)S(1)}, bf16[2,128,1024]{2,1,0:T(8,128)(2,1)}, u32[]{:S(2)}) copy-start(bf16[2,128,1024]{2,1,0:T(8,128)(2,1)} %param.10) | copy-start | bytes 1572868
  4.9 38.2 %all-to-all-start = ((bf16[32,16,1024]{2,1,0:T(8,128)(2,1)}), bf16[32,16,1024]{2,1,0:T(8,128)(2,1)}, u32[]{:S(2)}, u32[]{:S(2)}) async-start(bf16[32,16,1024]{2,1,0:T(8,128)(2,1)} %bitcast.30), calls=%async_computation | async-start | bytes 2097152 | tf_op jit(solution)/shard_map/all_to_all | solution.py:209
  43.1 30.0 %copy-start.1 = (bf16[2,1024,640]{2,1,0:T(8,128)(2,1)S(1)}, bf16[2,1024,640]{2,1,0:T(8,128)(2,1)}, u32[]{:S(2)}) copy-start(bf16[2,1024,640]{2,1,0:T(8,128)(2,1)} %refs_4_.3) | copy-start | bytes 7864324
  45.0 12.0 %collective-permute-start = (bf16[2,2,64,1024]{3,2,1,0:T(8,128)(2,1)S(1)}, bf16[2,2,64,1024]{3,2,1,0:T(8,128)(2,1)S(1)}, u32[]{:S(2)}, u32[]{:S(2)}) collective-permute-start(bf16[2,2,64,1024]{3,2,1,0:T(8,128)(2,1)S(1)} %get-tuple-element.40), channel_id=1, source_target_pairs={{0,1},{1,128},{128,129},{129,0},{2,3},{3,130},{130,131},{131,2},{4... | collective-permute-start | bytes 1572872 | tf_op jit(solution)/shard_map/ppermute | solution.py:201
  46.4 16.5 %collective-permute-start.1 = (bf16[2,2,64,1024]{3,2,1,0:T(8,128)(2,1)S(1)}, bf16[2,2,64,1024]{3,2,1,0:T(8,128)(2,1)S(1)}, u32[]{:S(2)}, u32[]{:S(2)}) collective-permute-start(bf16[2,2,64,1024]{3,2,1,0:T(8,128)(2,1)S(1)} %get-tuple-element.40), channel_id=1, source_target_pairs={{0,129},{1,0},{128,1},{129,128},{2,131},{3,2},{130,3},{131,130},{4... | collective-permute-start | bytes 1572872 | tf_op jit(solution)/shard_map/ppermute | solution.py:201
  47.9 23.4 %collective-permute-start.2 = (bf16[2,2,64,1024]{3,2,1,0:T(8,128)(2,1)S(1)}, bf16[2,2,64,1024]{3,2,1,0:T(8,128)(2,1)S(1)}, u32[]{:S(2)}, u32[]{:S(2)}) collective-permute-start(bf16[2,2,64,1024]{3,2,1,0:T(8,128)(2,1)S(1)} %get-tuple-element.39.refs_0_), channel_id=1, source_target_pairs={{0,128},{1,129},{128,0},{129,1},{2,130},{3,131},{130,2},{131,3},{4... | collective-permute-start | bytes 1572872 | tf_op jit(solution)/shard_map/ppermute | solution.py:201
  57.0 19.4 %collective-permute-start.3 = (bf16[2,2,64,1024]{3,2,1,0:T(8,128)(2,1)S(1)}, bf16[2,2,64,1024]{3,2,1,0:T(8,128)(2,1)S(1)}, u32[]{:S(2)}, u32[]{:S(2)}) collective-permute-start(bf16[2,2,64,1024]{3,2,1,0:T(8,128)(2,1)S(1)} %collective-permute-done.refs_1_), channel_id=1, source_target_pairs={{0,64},{64,0},{1,65},{65,1},{2,66},{66,2},{3,67},{67,3},{4,68},{68... | collective-permute-start | bytes 1572872 | tf_op jit(solution)/shard_map/ppermute | solution.py:205
  62.9 13.5 %collective-permute-start.4 = (bf16[2,2,64,1024]{3,2,1,0:T(8,128)(2,1)S(1)}, bf16[2,2,64,1024]{3,2,1,0:T(8,128)(2,1)S(1)}, u32[]{:S(2)}, u32[]{:S(2)}) collective-permute-start(bf16[2,2,64,1024]{3,2,1,0:T(8,128)(2,1)S(1)} %get-tuple-element.39.refs_0_), channel_id=1, source_target_pairs={{0,64},{64,0},{1,65},{65,1},{2,66},{66,2},{3,67},{67,3},{4,68},{68... | collective-permute-start | bytes 1572872 | tf_op jit(solution)/shard_map/ppermute | solution.py:205
  62.9 13.5 %collective-permute-start.5 = (bf16[2,2,64,1024]{3,2,1,0:T(8,128)(2,1)S(1)}, bf16[2,2,64,1024]{3,2,1,0:T(8,128)(2,1)S(1)}, u32[]{:S(2)}, u32[]{:S(2)}) collective-permute-start(bf16[2,2,64,1024]{3,2,1,0:T(8,128)(2,1)S(1)} %collective-permute-done.1.refs_2_), channel_id=1, source_target_pairs={{0,64},{64,0},{1,65},{65,1},{2,66},{66,2},{3,67},{67,3},{4,68},{68... | collective-permute-start | bytes 1572872 | tf_op jit(solution)/shard_map/ppermute | solution.py:205
  71.3 5.1 %collective-permute-start.6 = (bf16[2,2,64,1024]{3,2,1,0:T(8,128)(2,1)S(1)}, bf16[2,2,64,1024]{3,2,1,0:T(8,128)(2,1)S(1)}, u32[]{:S(2)}, u32[]{:S(2)}) collective-permute-start(bf16[2,2,64,1024]{3,2,1,0:T(8,128)(2,1)S(1)} %collective-permute-done.2.refs_3_), channel_id=1, source_target_pairs={{0,64},{64,0},{1,65},{65,1},{2,66},{66,2},{3,67},{67,3},{4,68},{68... | collective-permute-start | bytes 1572872 | tf_op jit(solution)/shard_map/ppermute | solution.py:205
  79.6 2.7 %collective-permute-start.7 = (bf16[4,2,64,1024]{3,2,1,0:T(8,128)(2,1)S(1)}, bf16[4,2,64,1024]{3,2,1,0:T(8,128)(2,1)S(1)}, u32[]{:S(2)}, u32[]{:S(2)}) collective-permute-start(bf16[4,2,64,1024]{3,2,1,0:T(8,128)(2,1)S(1)} %get-tuple-element.48), channel_id=1, source_target_pairs={{0,64},{64,0},{1,65},{65,1},{2,66},{66,2},{3,67},{67,3},{4,68},{68... | collective-permute-start | bytes 3145736 | tf_op jit(solution)/shard_map/ppermute | solution.py:205
  82.7 9.4 %collective-permute-start.10 = (bf16[2,64,1024]{2,1,0:T(8,128)(2,1)S(1)}, bf16[2,64,1024]{2,1,0:T(8,128)(2,1)S(1)}, u32[]{:S(2)}, u32[]{:S(2)}) collective-permute-start(bf16[2,64,1024]{2,1,0:T(8,128)(2,1)S(1)} %get-tuple-element.66), channel_id=1, source_target_pairs={{0,1},{1,128},{128,129},{129,0},{2,3},{3,130},{130,131},{131,2},{4... | collective-permute-start | bytes 786440 | tf_op jit(solution)/shard_map/ppermute | solution.py:201
  83.7 8.5 %collective-permute-start.9 = (bf16[2,64,1024]{2,1,0:T(8,128)(2,1)S(1)}, bf16[2,64,1024]{2,1,0:T(8,128)(2,1)S(1)}, u32[]{:S(2)}, u32[]{:S(2)}) collective-permute-start(bf16[2,64,1024]{2,1,0:T(8,128)(2,1)S(1)} %get-tuple-element.67), channel_id=1, source_target_pairs={{0,129},{1,0},{128,1},{129,128},{2,131},{3,2},{130,3},{131,130},{4... | collective-permute-start | bytes 786440 | tf_op jit(solution)/shard_map/ppermute | solution.py:201
  85.5 11.9 %collective-permute-start.8 = (bf16[2,64,1024]{2,1,0:T(8,128)(2,1)S(1)}, bf16[2,64,1024]{2,1,0:T(8,128)(2,1)S(1)}, u32[]{:S(2)}, u32[]{:S(2)}) collective-permute-start(bf16[2,64,1024]{2,1,0:T(8,128)(2,1)S(1)} %get-tuple-element.68), channel_id=1, source_target_pairs={{0,128},{1,129},{128,0},{129,1},{2,130},{3,131},{130,2},{131,3},{4... | collective-permute-start | bytes 786440 | tf_op jit(solution)/shard_map/ppermute | solution.py:201
  92.1 27.3 %copy-start.2 = (bf16[2,256,1024]{2,1,0:T(8,128)(2,1)S(1)}, bf16[2,256,1024]{2,1,0:T(8,128)(2,1)}, u32[]{:S(2)}) copy-start(bf16[2,256,1024]{2,1,0:T(8,128)(2,1)} %tokens_ref.1) | copy-start | bytes 3145732
  92.1 27.3 %copy-start.3 = (f32[2,256,128]{2,1,0:T(8,128)S(1)}, f32[2,256,128]{2,1,0:T(8,128)}, u32[]{:S(2)}) copy-start(f32[2,256,128]{2,1,0:T(8,128)} %get-tuple-element.57.dispatch_ref) | copy-start | bytes 786436
  97.7 32.1 %copy-start.4 = (bf16[1024,128]{1,0:T(8,128)(2,1)S(1)}, bf16[1024,128]{1,0:T(8,128)(2,1)}, u32[]{:S(2)}) copy-start(bf16[1024,128]{1,0:T(8,128)(2,1)} %params_ref.1) | copy-start | bytes 786436
  121.2 17.3 %all-to-all-start.2 = ((bf16[32,32,128]{2,1,0:T(8,128)(2,1)}), bf16[32,32,128]{2,1,0:T(8,128)(2,1)S(1)}, u32[]{:S(2)}, u32[]{:S(2)}) async-start(bf16[32,32,128]{2,1,0:T(8,128)(2,1)} %bitcast.9), calls=%async_computation.2 | async-start | bytes 524288 | tf_op jit(solution)/shard_map/all_to_all | solution.py:209
